TPU v7x, 256 devices: a whole 4x4x8 slice. The times are simulated.
256 devices in a mesh: facet: 8 (over x_hi, y), sub: 32 (over z, x_lo, core).
Axes of the slice: x: 4 (x_hi: 2, x_lo: 2; x = x_hi * 2 + x_lo), y: 4, z: 8, core: 2. Of those that a mesh axis runs over, the one named last changes fastest.
Arguments:
- facets: float32 [8, 2, 64, 2048], P('facet', None, 'sub'), may hold values from -6 to 6
- taper_weight: float32 [2048], replicated, may hold values from 0.5 to 1.5
- offsets: int32 [256], replicated, may hold values from 0 to 65535
- point_coords: float32 [2, 1048576], P(None, ('facet', 'sub')), may hold values from -32 to 32
- owners: int32 [1048576, 1], P(('facet', 'sub')), may hold values from 0 to 31; in each aligned block of 4096 rows (0 to 4095, 4096 to 8191, ...) at most 512 rows name the same one
Outputs:
- visibilities: float32 [2, 1048576], P(None, ('facet', 'sub'))
Inputs may be any that keep to these rules, and one draw needn't show every extreme that they name: `owners`: among the rows of one device no value is named by more than 512 rows, a bound that some block reaches.
All inputs are finite; a program needn't handle non-finite values.
Results may differ from a plain program's by a relative error of at most 0.0026.
Values may be sent and summed in bfloat16 or wider, within the bound.
No kernel may reach another device: no remote copies, remote signals or barrier semaphores. Data moves between devices by JAX's collectives and lax.ppermute only.
A program may use at most 128 MiB of HBM per device.

v0:
```python
import math

import jax
import jax.numpy as jnp
import ml_dtypes
import numpy as np
from jax import lax
from jax.experimental import pallas as pl
from jax.experimental.pallas import tpu as pltpu
from jax.sharding import PartitionSpec as P

N_IMG = 65536
XA = 256
ROWS = 64
SUBS = 32
CAP = 512
DEV_ROWS = 4096
F32 = jnp.float32
BF16 = jnp.bfloat16


def split_host(table):
    table = np.asarray(table, np.float32)
    high = table.astype(ml_dtypes.bfloat16)
    low = (table - high.astype(np.float32)).astype(ml_dtypes.bfloat16)
    return high, low


def transform_tables():
    turn = 2.0 * np.pi / 256.0
    a, q = np.arange(64), np.arange(256)
    first = np.outer(a, q) % 256 * turn
    real, imag = np.cos(first), -np.sin(first)
    outer = np.block([[real, imag], [-imag, real]])
    angle = np.outer(q, q) * (2.0 * np.pi / N_IMG)
    twiddle = np.stack([np.cos(angle), -np.sin(angle)]) / 128.0
    second = np.outer(q, q) % 256 * turn
    real, imag = np.cos(second), -np.sin(second)
    inner = np.block([[real, -imag], [imag, real]])
    return split_host(outer) + (twiddle.astype(np.float32),) + split_host(inner)


def fold_tables():
    order = []
    for h in range(8):
        order += [16 * h + 8 - l for l in range(8)] + [16 * h + 9 + l for l in range(8)]
    cells = np.zeros((XA, 2 * 128), np.float32)
    for place, m in enumerate(order):
        if m < 128:
            cells[128 + m, place] += 1.0
            cells[128 + m, 128 + place] += 1.0
        cells[128 - m, place] += 1.0
        cells[128 - m, 128 + place] -= 1.0
    order = []
    for h in range(2):
        order += [16 * h + 7 - l for l in range(8)] + [16 * h + 8 + l for l in range(8)]
    rows = np.zeros((ROWS, ROWS), np.float32)
    for place, k in enumerate(order):
        upper, lower = 32 + k, 31 - k
        upper_at = upper % 2 * SUBS + upper // 2
        lower_at = lower % 2 * SUBS + lower // 2
        rows[place, upper_at] = rows[place, lower_at] = 1.0
        rows[32 + place, upper_at], rows[32 + place, lower_at] = 1.0, -1.0
    return cells.astype(ml_dtypes.bfloat16), rows


def turn_polynomials():
    nodes = (np.cos(np.pi * (np.arange(400) + 0.5) / 400) + 1.0) / 8.0
    r = np.sqrt(nodes)
    fit = np.polynomial.chebyshev.Chebyshev.fit
    cosine = fit(nodes, np.cos(2 * np.pi * r), 7, domain=[0, 0.25])
    sine = fit(nodes, np.sin(2 * np.pi * r) / r, 6, domain=[0, 0.25])
    plain = np.polynomial.Polynomial
    return (
        [float(c) for c in cosine.convert(kind=plain).coef],
        [float(c) for c in sine.convert(kind=plain).coef],
    )


COS_TERMS, SIN_TERMS = turn_polynomials()


def unit_turns(turns):
    r = turns - jnp.round(turns)
    square = r * r
    cosine = jnp.full_like(square, COS_TERMS[-1])
    for term in COS_TERMS[-2::-1]:
        cosine = cosine * square + term
    sine = jnp.full_like(square, SIN_TERMS[-1])
    for term in SIN_TERMS[-2::-1]:
        sine = sine * square + term
    return cosine, sine * r


def pieces_of(values):
    first = values.astype(BF16)
    rest = values - first.astype(F32)
    second = rest.astype(BF16)
    third = (rest - second.astype(F32)).astype(BF16)
    return first, second, third


def iota(shape, axis):
    return lax.broadcasted_iota(jnp.int32, shape, axis)


def pack_kernel(coords_ref, owners_ref, packed_ref, position_ref):
    width = 256
    owner_of = iota((SUBS, width), 0)
    slot_of = iota((CAP, width), 0)
    upper = (iota((width, width), 0) <= iota((width, width), 1)).astype(BF16)
    carry = jnp.zeros((SUBS, 1), F32)
    total = jnp.zeros((6 * SUBS, CAP), F32)
    for block in range(DEV_ROWS // width):
        lanes = pl.ds(block * width, width)
        match = owners_ref[:, lanes] == owner_of
        hot = match.astype(F32)
        running = jnp.dot(hot.astype(BF16), upper, preferred_element_type=F32) + carry
        rank = jnp.sum(hot * running, axis=0, keepdims=True) - 1.0
        carry = carry + jnp.sum(hot, axis=1, keepdims=True)
        position = rank.astype(jnp.int32)
        position_ref[:, lanes] = position
        slots = (slot_of == position).astype(F32).astype(BF16)
        rows = []
        for axis in range(2):
            for piece in pieces_of(coords_ref[axis : axis + 1, lanes]):
                rows.append((hot * piece.astype(F32)).astype(BF16))
        total = total + lax.dot_general(
            jnp.concatenate(rows, axis=0),
            slots,
            (((1,), (1,)), ((), ())),
            preferred_element_type=F32,
        )
    for axis in range(2):
        at = 96 * axis
        values = total[at : at + 32] + (total[at + 32 : at + 64] + total[at + 64 : at + 96])
        packed_ref[:, 2 * axis, :] = values[:, :256]
        packed_ref[:, 2 * axis + 1, :] = values[:, 256:]


def split_dot(left_pair, right_pair):
    left_high, left_low = left_pair
    right_high, right_low = right_pair
    out = jnp.dot(left_high, right_high, preferred_element_type=F32)
    out = out + jnp.dot(left_low, right_high, preferred_element_type=F32)
    return out + jnp.dot(left_high, right_low, preferred_element_type=F32)


def split_in_kernel(values):
    high = values.astype(BF16)
    return high, (values - high.astype(F32)).astype(BF16)


def window_kernel(
    starts_ref, image_ref, packed_ref, outer_h, outer_l, twiddle_ref, inner_h, inner_l, out_ref, spectrum
):
    planes = []
    for r in range(2):
        stacked = jnp.concatenate(
            [image_ref[f, 2 * part + r] for part in range(2) for f in range(8)], axis=0
        )
        mixed = split_dot(split_in_kernel(stacked.T), (outer_h[...], outer_l[...]))
        real, imag = mixed[:, :256], mixed[:, 256:]
        turn_real, turn_imag = twiddle_ref[0], twiddle_ref[1]
        planes.append(
            jnp.concatenate(
                [real * turn_real - imag * turn_imag, real * turn_imag + imag * turn_real], axis=0
            )
        )
    for r in range(2):
        result = split_dot((inner_h[...], inner_l[...]), split_in_kernel(planes[r]))
        spectrum[:, r, :] = result[:256]
        spectrum[:, 2 + r, :] = result[256:]
    lane = iota((4, 256), 1)
    for s in range(SUBS):
        start = starts_ref[s]
        high = start // 256
        low = start % 256
        here = spectrum[high]
        following = spectrum[(high + 1) % 256]
        window = jnp.where(lane >= low, here, following)
        window = pltpu.roll(window, (256 - low) % 256, 1)
        window = window.astype(BF16).astype(F32)
        out_ref[s] = jnp.concatenate([window, packed_ref[s]], axis=0)


def degrid_kernel(arrived_ref, cells_ref, rows_ref, out_ref, weights, bias, phases):
    exact = lax.Precision.HIGHEST
    folded = []
    constant = []
    for part in range(2):
        grid = jnp.concatenate(
            [arrived_ref[:, 2 * part, :], arrived_ref[:, 2 * part + 1, :]], axis=0
        )
        by_cell = jnp.dot(grid.astype(BF16), cells_ref[...], preferred_element_type=F32)
        folded.append(jnp.dot(rows_ref[...], by_cell, precision=exact, preferred_element_type=F32))
        middle = jnp.dot(rows_ref[...], grid, precision=exact, preferred_element_type=F32)
        constant.append(middle[:, 128:129])
    (real, imag), (real_mid, imag_mid) = folded, constant
    even, odd = slice(0, 32), slice(32, 64)
    cosine, sine = slice(0, 128), slice(128, 256)
    groups = (
        (real[even, cosine], -imag[even, sine], real_mid[even]),
        (imag[odd, cosine], real[odd, sine], imag_mid[odd]),
        (imag[even, cosine], real[even, sine], imag_mid[even]),
        (real[odd, cosine], -imag[odd, sine], real_mid[odd]),
    )
    for number, (left, right, middle) in enumerate(groups):
        at = pl.ds(32 * number, 32)
        weights[at, :] = jnp.concatenate([left, right], axis=1).astype(BF16)
        bias[at, :] = jnp.broadcast_to(middle, (32, 256))

    step = iota((8, 256), 0).astype(F32)
    centre_scale = (16.0 * step + 8.5) * (1.0 / XA)
    offset_scale = (step + 0.5) * (1.0 / XA)
    row_scale = (step + 0.5) * (1.0 / ROWS)

    def chunk(source, half):
        v = arrived_ref[source, 4 + half : 5 + half, :]
        u = arrived_ref[source, 6 + half : 7 + half, :]
        centre_cos, centre_sin = unit_turns(u * centre_scale)
        offset_cos, offset_sin = unit_turns(u * offset_scale)
        row_cos, row_sin = unit_turns(v * row_scale)
        for h in range(8):
            a_cos, a_sin = centre_cos[h : h + 1], centre_sin[h : h + 1]
            cc, ss = a_cos * offset_cos, a_sin * offset_sin
            sc, cs = a_sin * offset_cos, a_cos * offset_sin
            at = 16 * h
            phases[half, at : at + 16, :] = jnp.concatenate([cc + ss, cc - ss], axis=0).astype(BF16)
            phases[half, 128 + at : 144 + at, :] = jnp.concatenate(
                [sc - cs, sc + cs], axis=0
            ).astype(BF16)
        inner = jnp.dot(weights[...], phases[half], preferred_element_type=F32) + bias[...]
        first_cos, first_sin = row_cos[0:1], row_sin[0:1]
        last_cos, last_sin = row_cos[7:8], row_sin[7:8]
        eight_cos = first_cos * last_cos - first_sin * last_sin
        eight_sin = first_cos * last_sin + first_sin * last_cos
        two_cos = eight_cos * eight_cos - eight_sin * eight_sin
        two_sin = 2.0 * eight_cos * eight_sin
        three_cos = eight_cos * two_cos - eight_sin * two_sin
        three_sin = eight_cos * two_sin + eight_sin * two_cos
        total_real = jnp.zeros((8, 256), F32)
        total_imag = jnp.zeros((8, 256), F32)
        for h, (a_cos, a_sin) in enumerate(((eight_cos, eight_sin), (three_cos, three_sin))):
            cc, ss = a_cos * row_cos, a_sin * row_sin
            sc, cs = a_sin * row_cos, a_cos * row_sin
            for side, (cosk, sink) in enumerate(((cc + ss, sc - cs), (cc - ss, sc + cs))):
                at = 16 * h + 8 * side
                total_real += inner[at : at + 8] * cosk - inner[32 + at : 40 + at] * sink
                total_imag += inner[64 + at : 72 + at] * cosk + inner[96 + at : 104 + at] * sink
        real_sum = jnp.sum(total_real, axis=0, keepdims=True) * (1.0 / 128.0)
        imag_sum = jnp.sum(total_imag, axis=0, keepdims=True) * (1.0 / 128.0)
        out_ref[source, half : half + 1, :] = real_sum * first_cos + imag_sum * first_sin
        out_ref[source, 2 + half : 3 + half, :] = imag_sum * first_cos - real_sum * first_sin

    def both(source, carry):
        chunk(source, 0)
        chunk(source, 1)
        return carry

    lax.fori_loop(0, SUBS, both, 0)


def unpack_kernel(returned_ref, owners_ref, position_ref, out_ref):
    rows = []
    for axis in range(2):
        values = jnp.concatenate(
            [returned_ref[:, 2 * axis, :], returned_ref[:, 2 * axis + 1, :]], axis=1
        )
        rows += list(pieces_of(values))
    table = jnp.concatenate(rows, axis=0)
    width = 512
    owner_of = iota((SUBS, width), 0)
    slot_of = iota((CAP, width), 0)
    for block in range(DEV_ROWS // width):
        lanes = pl.ds(block * width, width)
        match = owners_ref[:, lanes] == owner_of
        slots = (slot_of == position_ref[:, lanes]).astype(F32).astype(BF16)
        picked = jnp.dot(table, slots, preferred_element_type=F32)
        for axis in range(2):
            at = 96 * axis
            values = picked[at : at + 32] + (picked[at + 32 : at + 64] + picked[at + 64 : at + 96])
            out_ref[axis : axis + 1, lanes] = jnp.sum(
                jnp.where(match, values, 0.0), axis=0, keepdims=True
            )


def vmem():
    return pl.BlockSpec(memory_space=pltpu.VMEM)


def call(kernel, out_shape, in_specs, scratch, flops, *operands):
    return pl.pallas_call(
        kernel,
        out_shape=out_shape,
        in_specs=in_specs,
        out_specs=jax.tree.map(lambda _: vmem(), out_shape),
        scratch_shapes=scratch,
        compiler_params=pltpu.CompilerParams(vmem_limit_bytes=40 * 1024 * 1024),
        cost_estimate=pl.CostEstimate(flops=flops, bytes_accessed=1 << 20, transcendentals=0),
    )(*operands)


def per_device(facets, taper_weight, offsets, point_coords, owners):
    facet_index = lax.axis_index("facet")
    image = (facets[0] * taper_weight).reshape(4, 8, 256)
    image = lax.all_to_all(
        jnp.broadcast_to(image[None], (8, 4, 8, 256)), "facet", split_axis=0, concat_axis=0, tiled=True
    )
    owner_row = owners.reshape(1, DEV_ROWS)
    packed, position = call(
        pack_kernel,
        (
            jax.ShapeDtypeStruct((SUBS, 4, 256), F32),
            jax.ShapeDtypeStruct((1, DEV_ROWS), jnp.int32),
        ),
        [vmem()] * 2,
        [],
        1 << 32,
        point_coords,
        owner_row,
    )
    starts = lax.dynamic_slice(offsets, (facet_index * SUBS,), (SUBS,))
    outer_h, outer_l, twiddle, inner_h, inner_l = transform_tables()
    payload = call(
        window_kernel,
        jax.ShapeDtypeStruct((SUBS, 8, 256), F32),
        [pl.BlockSpec(memory_space=pltpu.SMEM)] + [vmem()] * 7,
        [pltpu.VMEM((256, 4, 256), F32)],
        1 << 32,
        starts,
        image,
        packed,
        outer_h,
        outer_l,
        twiddle,
        inner_h,
        inner_l,
    )
    arrived = lax.all_to_all(payload, "sub", split_axis=0, concat_axis=0, tiled=True)
    cells, rows = fold_tables()
    values = call(
        degrid_kernel,
        jax.ShapeDtypeStruct((SUBS, 4, 256), F32),
        [vmem()] * 3,
        [
            pltpu.VMEM((128, 256), BF16),
            pltpu.VMEM((128, 256), F32),
            pltpu.VMEM((2, 256, 256), BF16),
        ],
        1 << 32,
        arrived,
        cells,
        rows,
    )
    returned = lax.all_to_all(values, "sub", split_axis=0, concat_axis=0, tiled=True)
    return call(
        unpack_kernel,
        jax.ShapeDtypeStruct((2, DEV_ROWS), F32),
        [vmem()] * 3,
        [],
        1 << 32,
        returned,
        owner_row,
        position,
    )


def solution(mesh):
    placed = (
        P("facet", None, "sub", None),
        P(),
        P(),
        P(None, ("facet", "sub")),
        P(("facet", "sub"), None),
    )
    return jax.shard_map(
        per_device, mesh=mesh, in_specs=placed, out_specs=P(None, ("facet", "sub")), check_vma=False
    )
```

profile of v0, /device:TPU:1, one launch (start us, length us, event | category | flops | bytes accessed | tf_op | source)
XLA Modules:
  0.0 66.1 jit_solution(960674501949841205)
XLA Ops:
  0.0 0.0 copy-start.9
  0.0 0.8 %squeeze.3 = f32[4,8,256]{2,1,0:T(8,128)S(1)} reshape(f32[1,2,2,2048]{3,2,1,0:T(2,128)} %param.12) | data formatting | bytes 65536 | tf_op jit(solution)/shard_map/squeeze | solution.py:306
  0.8 0.0 copy-done.9
  0.8 0.7 %broadcast_in_dim.2 = f32[8,4,8,256]{3,2,1,0:T(8,128)} broadcast(f32[4,8,256]{2,1,0:T(8,128)S(1)} %broadcast_multiply_fusion), dimensions={1,2,3} | broadcast | bytes 294912 | tf_op jit(solution)/shard_map/broadcast_in_dim | solution.py:308
  1.6 0.0 copy-start.10
  1.6 0.0 copy-start
  1.6 7.6 %all-to-all-start = ((f32[8,4,8,256]{3,2,1,0:T(8,128)}), f32[8,4,8,256]{3,2,1,0:T(8,128)S(1)}, u32[]{:S(2)}, u32[]{:S(2)}) async-start(f32[8,4,8,256]{3,2,1,0:T(8,128)} %broadcast_in_dim.2), calls=%async_computation | async-start | bytes 524288 | tf_op jit(solution)/shard_map/all_to_all | solution.py:307
  9.2 0.0 copy-start.1
  9.2 0.0 copy-done.10
  9.2 0.1 dynamic_slice.3.starts_ref
  9.3 0.0 copy-done
  9.3 0.6 copy-done.1
  9.9 0.0 copy-start.2
  9.9 0.0 copy-start.3
  9.9 0.0 copy-start.4
  9.9 0.0 copy-start.6
  9.9 0.0 copy-start.7
  9.9 4.3 %shard_map.118 = (f32[32,4,256]{2,1,0:T(4,128)S(1)}, s32[1,4096]{1,0:T(1,128)S(1)}) custom-call(f32[2,4096]{1,0:T(2,128)S(1)} %copy-done, s32[1,4096]{1,0:T(1,128)S(1)} %bitcast.1), custom_call_target="tpu_custom_call" | custom-call | flops 4294967296 | bytes 1048576 | tf_op jit(solution)/shard_map/pallas_call | solution.py:293
  14.2 2.5 %all-to-all-done.image_ref = f32[8,4,8,256]{3,2,1,0:T(8,128)S(1)} async-done(((f32[8,4,8,256]{3,2,1,0:T(8,128)}), f32[8,4,8,256]{3,2,1,0:T(8,128)S(1)}, u32[]{:S(2)}, u32[]{:S(2)}) %all-to-all-start) | async-done | bytes 262176 | tf_op jit(solution)/shard_map/all_to_all | solution.py:307
  16.8 0.0 copy-done.2
  16.8 0.0 copy-done.3
  16.8 0.0 copy-done.4
  16.8 0.0 copy-done.6
  16.8 0.0 copy-done.7
  16.8 2.6 %shard_map.119 = f32[32,8,256]{2,1,0:T(8,128)S(1)} custom-call(s32[32]{0:T(128)S(1)} %dynamic_slice.3.starts_ref, f32[8,4,8,256]{3,2,1,0:T(8,128)S(1)} %all-to-all-done.image_ref, f32[32,4,256]{2,1,0:T(4,128)S(1)} %get-tuple-element.7.packed_ref, bf16[128,512]{1,0:T(8,128)(2,1)S(1)} %copy-done.6, bf16[128,512]{1,0:T(8,128)(2,1)S(1)} %copy-done.7, ...), custom_call_target="tpu_custom_call" | custom-call | flops 4294967296 | bytes 1048576 | tf_op jit(solution)/shard_map/pallas_call | solution.py:293
  19.4 0.0 copy-start.5
  19.4 0.0 copy-start.8
  19.4 22.1 %all_to_all.15.arrived_ref = f32[32,8,256]{2,1,0:T(8,128)S(1)} all-to-all(f32[32,8,256]{2,1,0:T(8,128)S(1)} %shard_map.119), channel_id=1, replica_groups=mesh['facet'=8,'sub'=32] {'sub'}, dimensions={0} | all-to-all | bytes 524288 | tf_op jit(solution)/shard_map/all_to_all | solution.py:340
  41.5 0.0 copy-done.5
  41.5 0.0 copy-done.8
  41.5 9.4 %shard_map.120 = f32[32,4,256]{2,1,0:T(4,128)S(1)} custom-call(f32[32,8,256]{2,1,0:T(8,128)S(1)} %all_to_all.15.arrived_ref, bf16[256,256]{1,0:T(8,128)(2,1)S(1)} %copy-done.5, f32[64,64]{1,0:T(8,128)S(1)} %copy-done.8), custom_call_target="tpu_custom_call" | custom-call | flops 4294967296 | bytes 1048576 | tf_op jit(solution)/shard_map/pallas_call | solution.py:293
  51.0 13.2 %all_to_all.16.returned_ref = f32[32,4,256]{2,1,0:T(4,128)S(1)} all-to-all(f32[32,4,256]{2,1,0:T(4,128)S(1)} %shard_map.120), channel_id=1, replica_groups=mesh['facet'=8,'sub'=32] {'sub'}, dimensions={0} | all-to-all | bytes 262144 | tf_op jit(solution)/shard_map/all_to_all | solution.py:356
  64.2 1.9 %shard_map.121 = f32[2,4096]{1,0:T(2,128)} custom-call(f32[32,4,256]{2,1,0:T(4,128)S(1)} %all_to_all.16.returned_ref, s32[1,4096]{1,0:T(1,128)S(1)} %bitcast.2, s32[1,4096]{1,0:T(1,128)S(1)} %get-tuple-element.8.position_ref), custom_call_target="tpu_custom_call" | custom-call | flops 4294967296 | bytes 1048576 | tf_op jit(solution)/shard_map/pallas_call | solution.py:293
  (2 shorter events, 0.0 us)
Async XLA Ops:
  0.0 0.8 %copy-start.9 = (f32[2048]{0:T(1024)S(1)}, f32[2048]{0:T(1024)}, u32[]{:S(2)}) copy-start(f32[2048]{0:T(1024)} %param.13) | copy-start | bytes 24580
  1.6 7.6 %copy-start.10 = (s32[256]{0:T(256)S(1)}, s32[256]{0:T(256)}, u32[]{:S(2)}) copy-start(s32[256]{0:T(256)} %param.14) | copy-start | bytes 3076
  1.6 7.7 %copy-start = (f32[2,4096]{1,0:T(2,128)S(1)}, f32[2,4096]{1,0:T(2,128)}, u32[]{:S(2)}) copy-start(f32[2,4096]{1,0:T(2,128)} %coords_ref.1) | copy-start | bytes 98308
  1.6 15.2 %all-to-all-start = ((f32[8,4,8,256]{3,2,1,0:T(8,128)}), f32[8,4,8,256]{3,2,1,0:T(8,128)S(1)}, u32[]{:S(2)}, u32[]{:S(2)}) async-start(f32[8,4,8,256]{3,2,1,0:T(8,128)} %broadcast_in_dim.2), calls=%async_computation | async-start | bytes 524288 | tf_op jit(solution)/shard_map/all_to_all | solution.py:307
  9.2 0.7 %copy-start.1 = (s32[4096,1]{0,1:T(1,128)S(1)}, s32[4096,1]{0,1:T(1,128)}, u32[]{:S(2)}) copy-start(s32[4096,1]{0,1:T(1,128)} %param.16) | copy-start | bytes 49156
  9.9 6.9 %copy-start.2 = (f32[2,256,256]{2,1,0:T(8,128)S(1)}, f32[2,256,256]{2,1,0:T(8,128)}, u32[]{:S(2)}) copy-start(f32[2,256,256]{2,1,0:T(8,128)} %constant.28.clone.twiddle_ref) | copy-start | bytes 1572868
  9.9 6.9 %copy-start.3 = (bf16[512,512]{1,0:T(8,128)(2,1)S(1)}, bf16[512,512]{1,0:T(8,128)(2,1)}, u32[]{:S(2)}) copy-start(bf16[512,512]{1,0:T(8,128)(2,1)} %constant.29.clone.inner_h) | copy-start | bytes 1572868
  9.9 6.9 %copy-start.4 = (bf16[512,512]{1,0:T(8,128)(2,1)S(1)}, bf16[512,512]{1,0:T(8,128)(2,1)}, u32[]{:S(2)}) copy-start(bf16[512,512]{1,0:T(8,128)(2,1)} %constant.30.clone.inner_l) | copy-start | bytes 1572868
  9.9 6.9 %copy-start.6 = (bf16[128,512]{1,0:T(8,128)(2,1)S(1)}, bf16[128,512]{1,0:T(8,128)(2,1)}, u32[]{:S(2)}) copy-start(bf16[128,512]{1,0:T(8,128)(2,1)} %constant.26.clone.outer_h) | copy-start | bytes 393220
  9.9 6.9 %copy-start.7 = (bf16[128,512]{1,0:T(8,128)(2,1)S(1)}, bf16[128,512]{1,0:T(8,128)(2,1)}, u32[]{:S(2)}) copy-start(bf16[128,512]{1,0:T(8,128)(2,1)} %constant.27.clone.outer_l) | copy-start | bytes 393220
  19.4 22.1 %copy-start.5 = (bf16[256,256]{1,0:T(8,128)(2,1)S(1)}, bf16[256,256]{1,0:T(8,128)(2,1)}, u32[]{:S(2)}) copy-start(bf16[256,256]{1,0:T(8,128)(2,1)} %constant.31.clone.cells_ref) | copy-start | bytes 393220
  19.4 22.1 %copy-start.8 = (f32[64,64]{1,0:T(8,128)S(1)}, f32[64,64]{1,0:T(8,128)}, u32[]{:S(2)}) copy-start(f32[64,64]{1,0:T(8,128)} %constant.32.clone.rows_ref) | copy-start | bytes 49156
where the time goes:
time: 66.5 us; the launch traced here: 66.1 us
  blocking collectives  35.3 us (53%)
  Pallas kernels  18.3 us (28%)
  starting transfers between devices  7.61 us (11%)
  waiting for transfers between devices  2.52 us (4%)
  local copies, waits for them, and re-layouts  2.26 us (3%)
    all_to_all x1, blocking collectives, per_device(): lax.all_to_all(payload, 'sub', split_axis=0, concat_axis=0, tiled=True)  22.1 us
    pallas_call x4, Pallas kernels, call(): pl.pallas_call(kernel, out_shape=out_shape, in_specs=in_specs, out_specs=...  18.3 us
    all_to_all x1, blocking collectives, per_device(): lax.all_to_all(values, 'sub', split_axis=0, concat_axis=0, tiled=True)  13.2 us
    all_to_all x1, starting transfers between devices, per_device(): lax.all_to_all(jnp.broadcast_to(image[None], (8, 4, 8, 256)), 'facet', sp...  7.61 us
    all_to_all x1, waiting for transfers between devices, per_device(): lax.all_to_all(jnp.broadcast_to(image[None], (8, 4, 8, 256)), 'facet', sp...  2.52 us
  transfers between devices with their start and end apart: 1, of which 1 were waited for; matrix products, arithmetic and copies ran while one was open for 0% of the time, Pallas kernels for 7%

commit v1 on v0

v1 whole, which is shorter than its diff:
```python
import math

import jax
import jax.numpy as jnp
import ml_dtypes
import numpy as np
from jax import lax
from jax.experimental import pallas as pl
from jax.experimental.pallas import tpu as pltpu
from jax.sharding import PartitionSpec as P

N_IMG = 65536
XA = 256
ROWS = 64
SUBS = 32
CAP = 512
DEV_ROWS = 4096
PARTS = 4
F32 = jnp.float32
BF16 = jnp.bfloat16


def split_host(table):
    table = np.asarray(table, np.float32)
    high = table.astype(ml_dtypes.bfloat16)
    low = (table - high.astype(np.float32)).astype(ml_dtypes.bfloat16)
    return high, low


def transform_tables():
    turn = 2.0 * np.pi / 256.0
    a, q = np.arange(64), np.arange(256)
    first = np.outer(a, q) % 256 * turn
    real, imag = np.cos(first), -np.sin(first)
    outer = np.block([[real, imag], [-imag, real]])
    angle = np.outer(q, q) * (2.0 * np.pi / N_IMG)
    twiddle = np.stack([np.cos(angle), -np.sin(angle)]) / 128.0
    second = np.outer(q, q) % 256 * turn
    real, imag = np.cos(second), -np.sin(second)
    inner = np.block([[real, -imag], [imag, real]])
    return split_host(outer) + (twiddle.astype(np.float32),) + split_host(inner)


def fold_tables():
    order = [16 * h + 1 + j for j in range(16) for h in range(8)]
    cells = np.zeros((XA, 3 * 128), np.float32)
    for place, m in enumerate(order):
        if m < 128:
            cells[128 + m, place] += 1.0
            cells[128 + m, 128 + place] += 1.0
        cells[128 - m, place] += 1.0
        cells[128 - m, 128 + place] -= 1.0
    cells[128, 256:] = 1.0
    order = [4 * g + j for j in range(4) for g in range(8)]
    even, odd = np.zeros((2, 32, ROWS), np.float32)
    for place, k in enumerate(order):
        for row, sign in ((32 + k, 1.0), (31 - k, -1.0)):
            at = row % 2 * SUBS + row // 2
            even[place, at], odd[place, at] = 1.0, sign
    none = np.zeros_like(even)
    with_cos = np.block([[even, none], [none, odd], [none, even], [odd, none]])
    with_sin = np.block([[none, -even], [odd, none], [even, none], [none, -odd]])
    return [table.astype(ml_dtypes.bfloat16) for table in (cells, with_cos, with_sin)]


def turn_polynomials(reach, cos_terms, sin_terms):
    nodes = (np.cos(np.pi * (np.arange(400) + 0.5) / 400) + 1.0) / 2.0 * reach**2
    r = np.sqrt(nodes)
    fit = np.polynomial.chebyshev.Chebyshev.fit
    cosine = fit(nodes, np.cos(2 * np.pi * r), cos_terms - 1, domain=[0, reach**2])
    sine = fit(nodes, np.sin(2 * np.pi * r) / r, sin_terms - 1, domain=[0, reach**2])
    plain = np.polynomial.Polynomial
    return (
        [float(c) for c in cosine.convert(kind=plain).coef],
        [float(c) for c in sine.convert(kind=plain).coef],
    )


ANY_TURN = turn_polynomials(0.5, 7, 6)
QUARTER_TURN = turn_polynomials(0.25, 5, 5)
SMALL_TURN = turn_polynomials(0.0625, 4, 3)


def reduced(turns):
    return turns - jnp.round(turns)


def unit_turns(r, terms):
    square = r * r
    cosine, sine = (jnp.full_like(square, part[-1]) for part in terms)
    for term in terms[0][-2::-1]:
        cosine = cosine * square + term
    for term in terms[1][-2::-1]:
        sine = sine * square + term
    return cosine, sine * r


def double_cos(half_step):
    return 2.0 - 4.0 * (half_step[1] * half_step[1])


def step_on(last, before, twice):
    return tuple(twice * x - y for x, y in zip(last, before))


def split_in_kernel(values):
    high = values.astype(BF16)
    return high, (values - high.astype(F32)).astype(BF16)


def iota(shape, axis):
    return lax.broadcasted_iota(jnp.int32, shape, axis)


def pack_kernel(coords_ref, owners_ref, packed_ref, position_ref):
    width = 256
    blocks = DEV_ROWS // width
    owner_of = iota((SUBS, width), 0)
    slot_of = iota((CAP, width), 0)
    upper = (iota((width, width), 0) <= iota((width, width), 1)).astype(F32).astype(BF16)
    hots = []
    for block in range(blocks):
        match = owners_ref[:, pl.ds(block * width, width)] == owner_of
        hots.append(match.astype(F32))
    running = jnp.dot(
        jnp.concatenate(hots, axis=0).astype(BF16), upper, preferred_element_type=F32
    )
    carry = jnp.zeros((SUBS, 1), F32)
    positions = []
    for block in range(blocks):
        mine = running[SUBS * block : SUBS * block + SUBS]
        rank = jnp.sum(hots[block] * (mine + carry), axis=0, keepdims=True) - 1.0
        carry = carry + mine[:, width - 1 : width]
        positions.append(rank.astype(jnp.int32))
        position_ref[:, pl.ds(block * width, width)] = positions[-1]
    total = jnp.zeros((4 * SUBS, CAP), F32)
    for block in range(blocks):
        lanes = pl.ds(block * width, width)
        slots = (slot_of == positions[block]).astype(F32).astype(BF16)
        rows = []
        for axis in range(2):
            for piece in split_in_kernel(coords_ref[axis : axis + 1, lanes]):
                rows.append((hots[block] * piece.astype(F32)).astype(BF16))
        total = total + lax.dot_general(
            jnp.concatenate(rows, axis=0),
            slots,
            (((1,), (1,)), ((), ())),
            preferred_element_type=F32,
        )
    for piece in range(4):
        for quarter in range(4):
            packed_ref[:, 4 * piece + quarter, :] = total[
                SUBS * piece : SUBS * piece + SUBS, 128 * quarter : 128 * quarter + 128
            ]


def split_dot(left_pair, right_pair):
    left_high, left_low = left_pair
    right_high, right_low = right_pair
    out = jnp.dot(left_high, right_high, preferred_element_type=F32)
    out = out + jnp.dot(left_low, right_high, preferred_element_type=F32)
    return out + jnp.dot(left_high, right_low, preferred_element_type=F32)


def spread_kernel(facets_ref, out_ref, rows):
    for part in range(2):
        for r in range(2):
            for block in range(16):
                at = 32 * part + 16 * r + block
                rows[at : at + 1, :] = facets_ref[
                    0, part, r : r + 1, 128 * block : 128 * block + 128
                ]
    for f in range(8):
        out_ref[f] = rows[...]


def window_kernel(
    starts_ref,
    image_ref,
    taper_ref,
    packed_ref,
    outer_h,
    outer_l,
    twiddle_ref,
    inner_h,
    inner_l,
    out_ref,
    columns,
    spectrum,
    payload,
):
    planes = []
    for r in range(2):
        for part in range(2):
            for f in range(8):
                for side in range(2):
                    line = image_ref[f, pl.ds(32 * part + 16 * r + side, 8, stride=2), :]
                    at = 64 * part + 8 * f
                    columns[r, at : at + 8, 128 * side : 128 * side + 128] = (
                        line * taper_ref[pl.ds(side, 8, stride=2), :]
                    )
        mixed = split_dot(split_in_kernel(columns[r].T), (outer_h[...], outer_l[...]))
        real, imag = mixed[:, :256], mixed[:, 256:]
        turn_real, turn_imag = twiddle_ref[0], twiddle_ref[1]
        planes.append(
            jnp.concatenate(
                [real * turn_real - imag * turn_imag, real * turn_imag + imag * turn_real], axis=0
            )
        )
    for r in range(2):
        result = split_dot((inner_h[...], inner_l[...]), split_in_kernel(planes[r]))
        spectrum[:, r, :] = result[:256]
        spectrum[:, 2 + r, :] = result[256:]
    lane = iota((4, 256), 1)
    for s in range(SUBS):
        start = starts_ref[s]
        high = start // 256
        low = start % 256
        here = spectrum[high]
        following = spectrum[(high + 1) % 256]
        window = jnp.where(lane >= low, here, following)
        window = pltpu.roll(window, (256 - low) % 256, 1)
        payload[s] = jnp.concatenate([window[:, :128], window[:, 128:], packed_ref[s]], axis=0)
    out_ref[...] = payload[...].astype(BF16)


def degrid_kernel(
    arrived_ref, cells_ref, with_cos_ref, with_sin_ref, out_ref, arrived, coords, weights, bias, partial, values, *buffers
):
    arrived[...] = arrived_ref[...].astype(F32)
    grid = jnp.concatenate(
        [
            jnp.concatenate([arrived[:, 4 * side + plane, :] for plane in range(4)], axis=0)
            for side in range(2)
        ],
        axis=1,
    )
    for axis in range(2):
        for quarter in range(4):
            at = 8 + 8 * axis + quarter
            coords[axis, quarter] = arrived[:, at, :] + arrived[:, at + 4, :]
    by_cell = jnp.dot(grid.astype(BF16), cells_ref[...], preferred_element_type=F32)
    high, low = split_in_kernel(by_cell)

    def fold(matrix, columns):
        return jnp.dot(matrix, high[:, columns], preferred_element_type=F32) + jnp.dot(
            matrix, low[:, columns], preferred_element_type=F32
        )

    weights[:, 0:128] = fold(with_cos_ref[...], slice(0, 128)).astype(BF16)
    weights[:, 128:256] = fold(with_sin_ref[...], slice(128, 256)).astype(BF16)
    bias[...] = fold(with_cos_ref[...], slice(256, 384))

    step_row = iota((8, 256), 0).astype(F32)
    cell_scale = (16.0 * step_row + 8.5) * (1.0 / XA)
    row_scale = (4.0 * step_row + 2.0) * (1.0 / ROWS)
    def place(step, part):
        return (step * PARTS + part) // 2, part % 2

    def beside(step, part, axis):
        source, half = place(step, part)
        where = jnp.concatenate(
            [
                jnp.broadcast_to(
                    coords[1 - axis, 2 * half + side, pl.ds(source, 1), :], (8, 128)
                )
                for side in range(2)
            ],
            axis=1,
        )
        scale, terms, centre_scale = (
            (0.5 / XA, SMALL_TURN, cell_scale),
            (0.5 / ROWS, QUARTER_TURN, row_scale),
        )[axis]
        a_cos, a_sin = unit_turns(reduced(where * centre_scale), ANY_TURN)
        b_cos, b_sin = unit_turns(where * scale, terms)
        cc, ss = a_cos * b_cos, a_sin * b_sin
        sc, cs = a_sin * b_cos, a_cos * b_sin
        return (cc + ss, sc - cs), (cc - ss, sc + cs), double_cos((b_cos, b_sin))

    def make_phases(step, part):
        below, above, twice = beside(step, part, 0)
        pieces = [[None] * 8, [None] * 8]
        for direction in (-1, 1):
            last, before, at = (below, above, 3) if direction < 0 else (above, below, 4)
            while True:
                following = step_on(last, before, twice)
                pair = (following, last) if direction < 0 else (last, following)
                for kind in range(2):
                    pieces[kind][at] = jnp.concatenate(
                        [pair[0][kind], pair[1][kind]], axis=0
                    ).astype(BF16)
                at += direction
                if not 0 <= at < 8:
                    break
                before, last = following, step_on(following, last, twice)
        return pieces[0] + pieces[1]

    def evaluate(step, part, inner):
        below, above, twice = beside(step, part, 1)
        total_real = total_imag = 0.0
        for j in (1, 0, 2, 3):
            if j == 0:
                cosk, sink = step_on(below, above, twice)
            elif j == 3:
                cosk, sink = step_on(above, below, twice)
            else:
                cosk, sink = below if j == 1 else above
            mine = []
            for at in range(8 * j, 8 * j + 128, 32):
                constant = bias[at : at + 8, :]
                mine.append(inner[at : at + 8] + jnp.concatenate([constant, constant], axis=1))
            total_real += mine[0] * cosk - mine[1] * sink
            total_imag += mine[2] * cosk + mine[3] * sink
        return total_real, total_imag

    steps = 2 * SUBS // PARTS

    def fill(made, buffer):
        for number, piece in enumerate(made):
            buffer[16 * number : 16 * number + 16, :] = piece

    def turn(step, ready, following):
        later = jnp.minimum(step + 1, steps - 1)
        inners = [
            jnp.dot(weights[...], ready[part][...], preferred_element_type=F32)
            for part in range(PARTS)
        ]
        made = [make_phases(later, part) for part in range(PARTS)]
        sums = [evaluate(step, part, inners[part]) for part in range(PARTS)]
        for part in range(PARTS):
            fill(made[part], following[part])
            source, half = place(step, part)
            for axis in range(2):
                partial[axis, half, source] = sums[part][axis]

    def both(pair, carry):
        turn(2 * pair, first, second)
        turn(2 * pair + 1, second, first)
        return carry

    first, second = buffers[:PARTS], buffers[PARTS:]
    for part in range(PARTS):
        fill(make_phases(0, part), first[part])
    lax.fori_loop(0, steps // 2, both, 0)
    for half in range(2):
        where = jnp.concatenate([coords[0, 2 * half], coords[0, 2 * half + 1]], axis=1)
        back_cos, back_sin = unit_turns(where * (0.5 / ROWS), QUARTER_TURN)
        real_sum, imag_sum = (
            sum(partial[axis, half, :, i, :] for i in range(8)) * (1.0 / 128.0) for axis in range(2)
        )
        for axis, value in enumerate(
            (real_sum * back_cos + imag_sum * back_sin, imag_sum * back_cos - real_sum * back_sin)
        ):
            at = 4 * axis + 2 * half
            values[:, at, :] = value[:, :128]
            values[:, at + 1, :] = value[:, 128:]
    out_ref[...] = values[...].astype(BF16)


def unpack_kernel(returned_ref, owners_ref, position_ref, out_ref, values):
    values[...] = returned_ref[...].astype(F32)
    table = jnp.concatenate(
        [
            jnp.concatenate([values[:, at, :], values[:, at + 1, :]], axis=1)
            for at in range(0, 8, 2)
        ],
        axis=0,
    ).astype(BF16)
    width = 512
    owner_of = iota((2 * SUBS, width), 0) % SUBS
    start_of = iota((2 * SUBS, width), 0) // SUBS * 256
    slot_of = iota((256, width), 0)
    for block in range(DEV_ROWS // width):
        lanes = pl.ds(block * width, width)
        position = position_ref[:, lanes]
        late = position // 256 * 256
        match = (owners_ref[:, lanes] == owner_of) & (late == start_of)
        slots = (slot_of == position - late).astype(F32).astype(BF16)
        picked = jnp.dot(table, slots, preferred_element_type=F32)
        for axis in range(2):
            out_ref[axis : axis + 1, lanes] = jnp.sum(
                jnp.where(match, picked[64 * axis : 64 * axis + 64], 0.0), axis=0, keepdims=True
            )


def vmem():
    return pl.BlockSpec(memory_space=pltpu.VMEM)


def call(kernel, out_shape, in_specs, scratch, flops, *operands):
    return pl.pallas_call(
        kernel,
        out_shape=out_shape,
        in_specs=in_specs,
        out_specs=jax.tree.map(lambda _: vmem(), out_shape),
        scratch_shapes=scratch,
        compiler_params=pltpu.CompilerParams(vmem_limit_bytes=40 * 1024 * 1024),
        cost_estimate=pl.CostEstimate(flops=flops, bytes_accessed=1 << 20, transcendentals=0),
    )(*operands)


def per_device(facets, taper_weight, offsets, point_coords, owners):
    facet_index = lax.axis_index("facet")
    image = call(
        spread_kernel,
        jax.ShapeDtypeStruct((8, 64, 128), F32),
        [vmem()],
        [pltpu.VMEM((64, 128), F32)],
        0,
        facets,
    )
    image = lax.all_to_all(image, "facet", split_axis=0, concat_axis=0, tiled=True)
    owner_row = owners.reshape(1, DEV_ROWS)
    packed, position = call(
        pack_kernel,
        (
            jax.ShapeDtypeStruct((SUBS, 16, 128), F32),
            jax.ShapeDtypeStruct((1, DEV_ROWS), jnp.int32),
        ),
        [vmem()] * 2,
        [],
        1 << 32,
        point_coords,
        owner_row,
    )
    starts = lax.dynamic_slice(offsets, (facet_index * SUBS,), (SUBS,))
    outer_h, outer_l, twiddle, inner_h, inner_l = transform_tables()
    payload = call(
        window_kernel,
        jax.ShapeDtypeStruct((SUBS, 24, 128), BF16),
        [pl.BlockSpec(memory_space=pltpu.SMEM)] + [vmem()] * 8,
        [
            pltpu.VMEM((2, 128, 256), F32),
            pltpu.VMEM((256, 4, 256), F32),
            pltpu.VMEM((SUBS, 24, 128), F32),
        ],
        1 << 32,
        starts,
        image,
        taper_weight.reshape(16, 128),
        packed,
        outer_h,
        outer_l,
        twiddle,
        inner_h,
        inner_l,
    )
    arrived = lax.all_to_all(payload, "sub", split_axis=0, concat_axis=0, tiled=True)
    values = call(
        degrid_kernel,
        jax.ShapeDtypeStruct((SUBS, 8, 128), BF16),
        [vmem()] * 4,
        [
            pltpu.VMEM((SUBS, 24, 128), F32),
            pltpu.VMEM((2, 4, SUBS, 128), F32),
            pltpu.VMEM((128, 256), BF16),
            pltpu.VMEM((128, 128), F32),
            pltpu.VMEM((2, 2, SUBS, 8, 256), F32),
            pltpu.VMEM((SUBS, 8, 128), F32),
        ]
        + [pltpu.VMEM((256, 256), BF16)] * (2 * PARTS),
        1 << 32,
        arrived,
        *fold_tables(),
    )
    returned = lax.all_to_all(values, "sub", split_axis=0, concat_axis=0, tiled=True)
    return call(
        unpack_kernel,
        jax.ShapeDtypeStruct((2, DEV_ROWS), F32),
        [vmem()] * 3,
        [pltpu.VMEM((SUBS, 8, 128), F32)],
        1 << 32,
        returned,
        owner_row,
        position,
    )


def solution(mesh):
    placed = (
        P("facet", None, "sub", None),
        P(),
        P(),
        P(None, ("facet", "sub")),
        P(("facet", "sub"), None),
    )
    return jax.shard_map(
        per_device, mesh=mesh, in_specs=placed, out_specs=P(None, ("facet", "sub")), check_vma=False
    )
```

time: 66.5 us -> 60.5 us (0.910)
  Pallas kernels: 18.3 us -> 13 us
  waiting for transfers between devices: 2.52 us -> 4.94 us
  blocking collectives: 35.3 us -> 33 us
  local copies, waits for them, and re-layouts: 2.26 us -> 1.51 us
    pallas_call x4 -> x5, Pallas kernels: 18.3 us -> 13 us  [call(): pl.pallas_call(kernel, out_shape=out_shape, in_specs=in_specs, out_specs=...]
    all_to_all x1, waiting for transfers between devices: 2.52 us -> 4.94 us  [per_device(): lax.all_to_all(image, 'facet', split_axis=0, concat_axis=0, tiled=True)]
    all_to_all x1, blocking collectives: 13.2 us -> 11.9 us  [per_device(): lax.all_to_all(values, 'sub', split_axis=0, concat_axis=0, tiled=True)]
    all_to_all x1, blocking collectives: 22.1 us -> 21 us  [per_device(): lax.all_to_all(payload, 'sub', split_axis=0, concat_axis=0, tiled=True)]
    squeeze x1 -> x0, local copies, waits for them, and re-layouts: 0.8 us -> none  [per_device(): image = (facets[0] * taper_weight).reshape(4, 8, 256)]
    unnamed x22 -> x26, local copies, waits for them, and re-layouts: 0.66 us -> 1.43 us
    broadcast_in_dim x1 -> x0, local copies, waits for them, and re-layouts: 0.72 us -> none  [per_device(): jnp.broadcast_to(image[None], (8, 4, 8, 256))]
  transfers between devices with their start and end apart: 1 -> 1, of which waited for: 1 -> 1; matrix products, arithmetic and copies ran while one was open for 0% -> 0% of each run, Pallas kernels for 7% -> 3%
where the time goes in v1:
time: 60.5 us; the launch traced here: 60.1 us
  blocking collectives  33 us (55%)
  Pallas kernels  13 us (21%)
  starting transfers between devices  7.61 us (13%)
  waiting for transfers between devices  4.94 us (8%)
  local copies, waits for them, and re-layouts  1.51 us (2%)
    all_to_all x1, blocking collectives, per_device(): lax.all_to_all(payload, 'sub', split_axis=0, concat_axis=0, tiled=True)  21 us
    pallas_call x5, Pallas kernels, call(): pl.pallas_call(kernel, out_shape=out_shape, in_specs=in_specs, out_specs=...  13 us
    all_to_all x1, blocking collectives, per_device(): lax.all_to_all(values, 'sub', split_axis=0, concat_axis=0, tiled=True)  11.9 us
    all_to_all x1, starting transfers between devices, per_device(): lax.all_to_all(image, 'facet', split_axis=0, concat_axis=0, tiled=True)  7.61 us
    all_to_all x1, waiting for transfers between devices, per_device(): lax.all_to_all(image, 'facet', split_axis=0, concat_axis=0, tiled=True)  4.94 us
    unnamed x26, local copies, waits for them, and re-layouts  1.43 us
  transfers between devices with their start and end apart: 1, of which 1 were waited for; matrix products, arithmetic and copies ran while one was open for 0% of the time, Pallas kernels for 3%

profile of v1, /device:TPU:1, one launch (start us, length us, event | category | flops | bytes accessed | tf_op | source)
XLA Modules:
  0.0 60.1 jit_solution(18301152825111139164)
XLA Ops:
  0.0 0.0 copy-start
  0.0 0.8 %copy-done = f32[1,2,2,2048]{3,2,1,0:T(2,128)S(1)} copy-done((f32[1,2,2,2048]{3,2,1,0:T(2,128)S(1)}, f32[1,2,2,2048]{3,2,1,0:T(2,128)}, u32[]{:S(2)}) %copy-start) | copy-done | bytes 32792
  0.8 0.7 %shard_map.127 = f32[8,64,128]{2,1,0:T(8,128)} custom-call(f32[1,2,2,2048]{3,2,1,0:T(2,128)S(1)} %copy-done), custom_call_target="tpu_custom_call" | custom-call | bytes 1048576 | tf_op jit(solution)/shard_map/pallas_call | solution.py:392
  1.5 0.0 copy-start.12
  1.5 0.0 copy-start.1
  1.5 7.6 %all-to-all-start = ((f32[8,64,128]{2,1,0:T(8,128)}), f32[8,64,128]{2,1,0:T(8,128)S(1)}, u32[]{:S(2)}, u32[]{:S(2)}) async-start(f32[8,64,128]{2,1,0:T(8,128)} %shard_map.127), calls=%async_computation | async-start | bytes 524288 | tf_op jit(solution)/shard_map/all_to_all | solution.py:413
  9.1 0.0 copy-start.2
  9.1 0.0 copy-done.12
  9.1 0.1 dynamic_slice.3.starts_ref
  9.2 0.0 copy-done.1
  9.2 0.6 %copy-done.2 = s32[4096,1]{0,1:T(1,128)S(1)} copy-done((s32[4096,1]{0,1:T(1,128)S(1)}, s32[4096,1]{0,1:T(1,128)}, u32[]{:S(2)}) %copy-start.2) | copy-done | bytes 16408
  9.8 0.0 copy-start.3
  9.8 0.0 copy-start.4
  9.8 0.0 copy-start.5
  9.8 0.0 copy-start.6
  9.8 0.0 copy-start.8
  9.9 0.0 copy-start.9
  9.9 1.9 %shard_map.128 = (f32[32,16,128]{2,1,0:T(8,128)S(1)}, s32[1,4096]{1,0:T(1,128)S(1)}) custom-call(f32[2,4096]{1,0:T(2,128)S(1)} %copy-done.1, s32[1,4096]{1,0:T(1,128)S(1)} %bitcast.2), custom_call_target="tpu_custom_call" | custom-call | flops 4294967296 | bytes 1048576 | tf_op jit(solution)/shard_map/pallas_call | solution.py:392
  11.8 4.9 %all-to-all-done.image_ref = f32[8,64,128]{2,1,0:T(8,128)S(1)} async-done(((f32[8,64,128]{2,1,0:T(8,128)}), f32[8,64,128]{2,1,0:T(8,128)S(1)}, u32[]{:S(2)}, u32[]{:S(2)}) %all-to-all-start) | async-done | bytes 262176 | tf_op jit(solution)/shard_map/all_to_all | solution.py:413
  16.7 0.0 copy-done.3
  16.7 0.0 copy-done.4
  16.7 0.0 copy-done.5
  16.7 0.0 copy-done.6
  16.7 0.0 copy-done.8
  16.7 0.0 copy-done.9
  16.7 2.6 %shard_map.129 = bf16[32,24,128]{2,1,0:T(8,128)(2,1)S(1)} custom-call(s32[32]{0:T(128)S(1)} %dynamic_slice.3.starts_ref, f32[8,64,128]{2,1,0:T(8,128)S(1)} %all-to-all-done.image_ref, f32[16,128]{1,0:T(8,128)S(1)} %bitcast.4, f32[32,16,128]{2,1,0:T(8,128)S(1)} %get-tuple-element.7.packed_ref, bf16[128,512]{1,0:T(8,128)(2,1)S(1)} %copy-done.9, ...), custom_call_target="tpu_custom_call" | custom-call | flops 4294967296 | bytes 1048576 | tf_op jit(solution)/shard_map/pallas_call | solution.py:392
  19.4 0.0 copy-start.7
  19.4 0.0 copy-start.10
  19.4 0.0 copy-start.11
  19.4 21.0 %all_to_all.15.arrived_ref = bf16[32,24,128]{2,1,0:T(8,128)(2,1)S(1)} all-to-all(bf16[32,24,128]{2,1,0:T(8,128)(2,1)S(1)} %shard_map.129), channel_id=1, replica_groups=mesh['facet'=8,'sub'=32] {'sub'}, dimensions={0} | all-to-all | bytes 393216 | tf_op jit(solution)/shard_map/all_to_all | solution.py:449
  40.4 0.0 copy-done.7
  40.4 0.0 copy-done.10
  40.4 0.0 copy-done.11
  40.4 6.2 %shard_map.130 = bf16[32,8,128]{2,1,0:T(8,128)(2,1)S(1)} custom-call(bf16[32,24,128]{2,1,0:T(8,128)(2,1)S(1)} %all_to_all.15.arrived_ref, bf16[256,384]{1,0:T(8,128)(2,1)S(1)} %copy-done.7, bf16[128,128]{1,0:T(8,128)(2,1)S(1)} %copy-done.11, bf16[128,128]{1,0:T(8,128)(2,1)S(1)} %copy-done.10), custom_call_target="tpu_custom_call" | custom-call | flops 4294967296 | bytes 1048576 | tf_op jit(solution)/shard_map/pallas_call | solution.py:392
  46.6 11.9 %all_to_all.16.returned_ref = bf16[32,8,128]{2,1,0:T(8,128)(2,1)S(1)} all-to-all(bf16[32,8,128]{2,1,0:T(8,128)(2,1)S(1)} %shard_map.130), channel_id=1, replica_groups=mesh['facet'=8,'sub'=32] {'sub'}, dimensions={0} | all-to-all | bytes 131072 | tf_op jit(solution)/shard_map/all_to_all | solution.py:467
  58.6 1.5 %shard_map.131 = f32[2,4096]{1,0:T(2,128)} custom-call(bf16[32,8,128]{2,1,0:T(8,128)(2,1)S(1)} %all_to_all.16.returned_ref, s32[1,4096]{1,0:T(1,128)S(1)} %bitcast.3, s32[1,4096]{1,0:T(1,128)S(1)} %get-tuple-element.8.position_ref), custom_call_target="tpu_custom_call" | custom-call | flops 4294967296 | bytes 1048576 | tf_op jit(solution)/shard_map/pallas_call | solution.py:392
Async XLA Ops:
  0.0 0.8 %copy-start = (f32[1,2,2,2048]{3,2,1,0:T(2,128)S(1)}, f32[1,2,2,2048]{3,2,1,0:T(2,128)}, u32[]{:S(2)}) copy-start(f32[1,2,2,2048]{3,2,1,0:T(2,128)} %facets_ref.1) | copy-start | bytes 98308
  1.5 7.6 %copy-start.12 = (s32[256]{0:T(256)S(1)}, s32[256]{0:T(256)}, u32[]{:S(2)}) copy-start(s32[256]{0:T(256)} %param.15) | copy-start | bytes 3076
  1.5 7.7 %copy-start.1 = (f32[2,4096]{1,0:T(2,128)S(1)}, f32[2,4096]{1,0:T(2,128)}, u32[]{:S(2)}) copy-start(f32[2,4096]{1,0:T(2,128)} %coords_ref.1) | copy-start | bytes 98308
  1.5 15.2 %all-to-all-start = ((f32[8,64,128]{2,1,0:T(8,128)}), f32[8,64,128]{2,1,0:T(8,128)S(1)}, u32[]{:S(2)}, u32[]{:S(2)}) async-start(f32[8,64,128]{2,1,0:T(8,128)} %shard_map.127), calls=%async_computation | async-start | bytes 524288 | tf_op jit(solution)/shard_map/all_to_all | solution.py:413
  9.1 0.7 %copy-start.2 = (s32[4096,1]{0,1:T(1,128)S(1)}, s32[4096,1]{0,1:T(1,128)}, u32[]{:S(2)}) copy-start(s32[4096,1]{0,1:T(1,128)} %param.17) | copy-start | bytes 49156
  9.8 6.9 %copy-start.3 = (f32[2048]{0:T(1024)S(1)}, f32[2048]{0:T(1024)}, u32[]{:S(2)}) copy-start(f32[2048]{0:T(1024)} %param.14) | copy-start | bytes 24580
  9.8 6.9 %copy-start.4 = (bf16[512,512]{1,0:T(8,128)(2,1)S(1)}, bf16[512,512]{1,0:T(8,128)(2,1)}, u32[]{:S(2)}) copy-start(bf16[512,512]{1,0:T(8,128)(2,1)} %constant.32.clone.inner_l) | copy-start | bytes 1572868
  9.8 6.9 %copy-start.5 = (bf16[512,512]{1,0:T(8,128)(2,1)S(1)}, bf16[512,512]{1,0:T(8,128)(2,1)}, u32[]{:S(2)}) copy-start(bf16[512,512]{1,0:T(8,128)(2,1)} %constant.31.clone.inner_h) | copy-start | bytes 1572868
  9.8 6.9 %copy-start.6 = (f32[2,256,256]{2,1,0:T(8,128)S(1)}, f32[2,256,256]{2,1,0:T(8,128)}, u32[]{:S(2)}) copy-start(f32[2,256,256]{2,1,0:T(8,128)} %constant.30.clone.twiddle_ref) | copy-start | bytes 1572868
  9.8 6.9 %copy-start.8 = (bf16[128,512]{1,0:T(8,128)(2,1)S(1)}, bf16[128,512]{1,0:T(8,128)(2,1)}, u32[]{:S(2)}) copy-start(bf16[128,512]{1,0:T(8,128)(2,1)} %constant.29.clone.outer_l) | copy-start | bytes 393220
  9.9 6.9 %copy-start.9 = (bf16[128,512]{1,0:T(8,128)(2,1)S(1)}, bf16[128,512]{1,0:T(8,128)(2,1)}, u32[]{:S(2)}) copy-start(bf16[128,512]{1,0:T(8,128)(2,1)} %constant.28.clone.outer_h) | copy-start | bytes 393220
  19.4 21.1 %copy-start.7 = (bf16[256,384]{1,0:T(8,128)(2,1)S(1)}, bf16[256,384]{1,0:T(8,128)(2,1)}, u32[]{:S(2)}) copy-start(bf16[256,384]{1,0:T(8,128)(2,1)} %constant.33.clone.cells_ref) | copy-start | bytes 589828
  19.4 21.1 %copy-start.10 = (bf16[128,128]{1,0:T(8,128)(2,1)S(1)}, bf16[128,128]{1,0:T(8,128)(2,1)}, u32[]{:S(2)}) copy-start(bf16[128,128]{1,0:T(8,128)(2,1)} %constant.35.clone.with_sin_ref) | copy-start | bytes 98308
  19.4 21.0 %copy-start.11 = (bf16[128,128]{1,0:T(8,128)(2,1)S(1)}, bf16[128,128]{1,0:T(8,128)(2,1)}, u32[]{:S(2)}) copy-start(bf16[128,128]{1,0:T(8,128)(2,1)} %constant.34.clone.with_cos_ref) | copy-start | bytes 98308

commit v2 on v1

--- a/solution.py
+++ b/solution.py
@@ -37,8 +37,8 @@
     twiddle = np.stack([np.cos(angle), -np.sin(angle)]) / 128.0
     second = np.outer(q, q) % 256 * turn
     real, imag = np.cos(second), -np.sin(second)
-    inner = np.block([[real, -imag], [imag, real]])
-    return split_host(outer) + (twiddle.astype(np.float32),) + split_host(inner)
+    inner = np.stack([real, imag], axis=1).astype(np.float32)
+    return inner, split_host(outer) + (twiddle.astype(np.float32),)
 
 
 def fold_tables():
@@ -112,7 +112,14 @@
     return lax.broadcasted_iota(jnp.int32, shape, axis)
 
 
-def pack_kernel(coords_ref, owners_ref, packed_ref, position_ref):
+def pack_kernel(
+    starts_ref, coords_ref, owners_ref, inner_ref, packed_ref, position_ref, high_ref, low_ref, chosen
+):
+    for s in range(SUBS):
+        run = starts_ref[s] // 256
+        chosen[4 * s : 4 * s + 2, :] = inner_ref[run]
+        chosen[4 * s + 2 : 4 * s + 4, :] = inner_ref[(run + 1) % 256]
+    high_ref[...], low_ref[...] = split_in_kernel(chosen[...])
     width = 256
     blocks = DEV_ROWS // width
     owner_of = iota((SUBS, width), 0)
@@ -179,17 +186,17 @@
     image_ref,
     taper_ref,
     packed_ref,
+    chosen_h,
+    chosen_l,
     outer_h,
     outer_l,
     twiddle_ref,
-    inner_h,
-    inner_l,
     out_ref,
     columns,
-    spectrum,
     payload,
 ):
-    planes = []
+    payload[:, 8:24, :] = packed_ref[...]
+    reals, imags = [], []
     for r in range(2):
         for part in range(2):
             for f in range(8):
@@ -202,25 +209,21 @@
         mixed = split_dot(split_in_kernel(columns[r].T), (outer_h[...], outer_l[...]))
         real, imag = mixed[:, :256], mixed[:, 256:]
         turn_real, turn_imag = twiddle_ref[0], twiddle_ref[1]
-        planes.append(
-            jnp.concatenate(
-                [real * turn_real - imag * turn_imag, real * turn_imag + imag * turn_real], axis=0
-            )
-        )
-    for r in range(2):
-        result = split_dot((inner_h[...], inner_l[...]), split_in_kernel(planes[r]))
-        spectrum[:, r, :] = result[:256]
-        spectrum[:, 2 + r, :] = result[256:]
-    lane = iota((4, 256), 1)
+        reals.append(real * turn_real - imag * turn_imag)
+        imags.append(real * turn_imag + imag * turn_real)
+    both = jnp.concatenate(reals + imags, axis=1)
+    runs = split_dot((chosen_h[...], chosen_l[...]), split_in_kernel(both))
+    lane = iota((2, 1024), 1) % 256
     for s in range(SUBS):
-        start = starts_ref[s]
-        high = start // 256
-        low = start % 256
-        here = spectrum[high]
-        following = spectrum[(high + 1) % 256]
-        window = jnp.where(lane >= low, here, following)
+        low = starts_ref[s] % 256
+        mine = runs[4 * s : 4 * s + 4]
+        mine = jnp.where(lane >= low, mine[0:2], mine[2:4])
+        real = mine[0:1, :512] - mine[1:2, 512:]
+        imag = mine[1:2, :512] + mine[0:1, 512:]
+        window = jnp.concatenate([real[:, :256], real[:, 256:], imag[:, :256], imag[:, 256:]], axis=0)
         window = pltpu.roll(window, (256 - low) % 256, 1)
-        payload[s] = jnp.concatenate([window[:, :128], window[:, 128:], packed_ref[s]], axis=0)
+        payload[s, 0:4, :] = window[:, :128]
+        payload[s, 4:8, :] = window[:, 128:]
     out_ref[...] = payload[...].astype(BF16)
 
 
@@ -388,6 +391,10 @@
     return pl.BlockSpec(memory_space=pltpu.VMEM)
 
 
+def smem():
+    return pl.BlockSpec(memory_space=pltpu.SMEM)
+
+
 def call(kernel, out_shape, in_specs, scratch, flops, *operands):
     return pl.pallas_call(
         kernel,
@@ -412,39 +419,37 @@
     )
     image = lax.all_to_all(image, "facet", split_axis=0, concat_axis=0, tiled=True)
     owner_row = owners.reshape(1, DEV_ROWS)
-    packed, position = call(
+    starts = lax.dynamic_slice(offsets, (facet_index * SUBS,), (SUBS,))
+    inner, tables = transform_tables()
+    packed, position, chosen_h, chosen_l = call(
         pack_kernel,
         (
             jax.ShapeDtypeStruct((SUBS, 16, 128), F32),
             jax.ShapeDtypeStruct((1, DEV_ROWS), jnp.int32),
+            jax.ShapeDtypeStruct((128, 256), BF16),
+            jax.ShapeDtypeStruct((128, 256), BF16),
         ),
-        [vmem()] * 2,
-        [],
+        [smem()] + [vmem()] * 3,
+        [pltpu.VMEM((128, 256), F32)],
         1 << 32,
+        starts,
         point_coords,
         owner_row,
-    )
-    starts = lax.dynamic_slice(offsets, (facet_index * SUBS,), (SUBS,))
-    outer_h, outer_l, twiddle, inner_h, inner_l = transform_tables()
+        inner,
+    )
     payload = call(
         window_kernel,
         jax.ShapeDtypeStruct((SUBS, 24, 128), BF16),
-        [pl.BlockSpec(memory_space=pltpu.SMEM)] + [vmem()] * 8,
-        [
-            pltpu.VMEM((2, 128, 256), F32),
-            pltpu.VMEM((256, 4, 256), F32),
-            pltpu.VMEM((SUBS, 24, 128), F32),
-        ],
+        [smem()] + [vmem()] * 8,
+        [pltpu.VMEM((2, 128, 256), F32), pltpu.VMEM((SUBS, 24, 128), F32)],
         1 << 32,
         starts,
         image,
         taper_weight.reshape(16, 128),
         packed,
-        outer_h,
-        outer_l,
-        twiddle,
-        inner_h,
-        inner_l,
+        chosen_h,
+        chosen_l,
+        *tables,
     )
     arrived = lax.all_to_all(payload, "sub", split_axis=0, concat_axis=0, tiled=True)
     values = call(

time: 60.5 us -> 59.6 us (0.985)
    unnamed x26 -> x24, local copies, waits for them, and re-layouts: 1.43 us -> 1.42 us
  transfers between devices with their start and end apart: 1 -> 1, of which waited for: 1 -> 1; matrix products, arithmetic and copies ran while one was open for 0% -> 0% of each run, Pallas kernels for 3% -> 4%
where the time goes in v2:
time: 59.6 us; the launch traced here: 59.2 us
  blocking collectives  33 us (55%)
  Pallas kernels  12.6 us (21%)
  starting transfers between devices  7.61 us (13%)
  waiting for transfers between devices  4.4 us (7%)
  local copies, waits for them, and re-layouts  1.5 us (3%)
    all_to_all x1, blocking collectives, per_device(): lax.all_to_all(payload, 'sub', split_axis=0, concat_axis=0, tiled=True)  21 us
    pallas_call x5, Pallas kernels, call(): pl.pallas_call(kernel, out_shape=out_shape, in_specs=in_specs, out_specs=...  12.6 us
    all_to_all x1, blocking collectives, per_device(): lax.all_to_all(values, 'sub', split_axis=0, concat_axis=0, tiled=True)  11.9 us
    all_to_all x1, starting transfers between devices, per_device(): lax.all_to_all(image, 'facet', split_axis=0, concat_axis=0, tiled=True)  7.61 us
    all_to_all x1, waiting for transfers between devices, per_device(): lax.all_to_all(image, 'facet', split_axis=0, concat_axis=0, tiled=True)  4.4 us
    unnamed x24, local copies, waits for them, and re-layouts  1.42 us
  transfers between devices with their start and end apart: 1, of which 1 were waited for; matrix products, arithmetic and copies ran while one was open for 0% of the time, Pallas kernels for 4%

profile of v2, /device:TPU:1, one launch (start us, length us, event | category | flops | bytes accessed | tf_op | source)
XLA Modules:
  0.0 59.2 jit_solution(14282146706572984574)
XLA Ops:
  0.0 0.0 copy-start
  0.0 0.8 %copy-done = f32[1,2,2,2048]{3,2,1,0:T(2,128)S(1)} copy-done((f32[1,2,2,2048]{3,2,1,0:T(2,128)S(1)}, f32[1,2,2,2048]{3,2,1,0:T(2,128)}, u32[]{:S(2)}) %copy-start) | copy-done | bytes 32792
  0.8 0.0 copy-start.5
  0.8 0.7 %shard_map.118 = f32[8,64,128]{2,1,0:T(8,128)} custom-call(f32[1,2,2,2048]{3,2,1,0:T(2,128)S(1)} %copy-done), custom_call_target="tpu_custom_call" | custom-call | bytes 1048576 | tf_op jit(solution)/shard_map/pallas_call | solution.py:399
  1.5 0.0 copy-start.11
  1.5 0.0 copy-start.1
  1.5 7.6 %all-to-all-start = ((f32[8,64,128]{2,1,0:T(8,128)}), f32[8,64,128]{2,1,0:T(8,128)S(1)}, u32[]{:S(2)}, u32[]{:S(2)}) async-start(f32[8,64,128]{2,1,0:T(8,128)} %shard_map.118), calls=%async_computation | async-start | bytes 524288 | tf_op jit(solution)/shard_map/all_to_all | solution.py:420
  9.1 0.0 copy-start.2
  9.1 0.0 copy-done.11
  9.1 0.1 dynamic_slice.3.starts_ref
  9.2 0.0 copy-done.5
  9.2 0.0 copy-done.1
  9.2 0.6 %copy-done.2 = s32[4096,1]{0,1:T(1,128)S(1)} copy-done((s32[4096,1]{0,1:T(1,128)S(1)}, s32[4096,1]{0,1:T(1,128)}, u32[]{:S(2)}) %copy-start.2) | copy-done | bytes 16408
  9.8 0.0 copy-start.3
  9.8 0.0 copy-start.4
  9.8 0.0 copy-start.7
  9.8 0.0 copy-start.8
  9.9 2.4 %shard_map.119 = (f32[32,16,128]{2,1,0:T(8,128)S(1)}, s32[1,4096]{1,0:T(1,128)S(1)}, bf16[128,256]{1,0:T(8,128)(2,1)S(1)}, bf16[128,256]{1,0:T(8,128)(2,1)S(1)}) custom-call(s32[32]{0:T(128)S(1)} %dynamic_slice.3.starts_ref, f32[2,4096]{1,0:T(2,128)S(1)} %copy-done.1, s32[1,4096]{1,0:T(1,128)S(1)} %bitcast.2, f32[256,2,256]{2,1,0:T(2,128)S(1)} %copy-done.5), custom_call_target="tpu_custom_call" | custom-call | flops 4294967296 | bytes 1048576 | tf_op jit(solution)/shard_map/pallas_call | solution.py:399
  12.3 4.4 %all-to-all-done.image_ref = f32[8,64,128]{2,1,0:T(8,128)S(1)} async-done(((f32[8,64,128]{2,1,0:T(8,128)}), f32[8,64,128]{2,1,0:T(8,128)S(1)}, u32[]{:S(2)}, u32[]{:S(2)}) %all-to-all-start) | async-done | bytes 262176 | tf_op jit(solution)/shard_map/all_to_all | solution.py:420
  16.7 0.0 copy-done.3
  16.7 0.0 copy-done.4
  16.7 0.0 copy-done.7
  16.7 0.0 copy-done.8
  16.7 1.7 %shard_map.120 = bf16[32,24,128]{2,1,0:T(8,128)(2,1)S(1)} custom-call(s32[32]{0:T(128)S(1)} %dynamic_slice.3.starts_ref, f32[8,64,128]{2,1,0:T(8,128)S(1)} %all-to-all-done.image_ref, f32[16,128]{1,0:T(8,128)S(1)} %bitcast.4, f32[32,16,128]{2,1,0:T(8,128)S(1)} %get-tuple-element.9.packed_ref, bf16[128,256]{1,0:T(8,128)(2,1)S(1)} %get-tuple-element.10.chosen_h, ...), custom_call_target="tpu_custom_call" | custom-call | flops 4294967296 | bytes 1048576 | tf_op jit(solution)/shard_map/pallas_call | solution.py:399
  18.5 0.0 copy-start.6
  18.5 0.0 copy-start.9
  18.5 0.0 copy-start.10
  18.5 21.0 %all_to_all.15.arrived_ref = bf16[32,24,128]{2,1,0:T(8,128)(2,1)S(1)} all-to-all(bf16[32,24,128]{2,1,0:T(8,128)(2,1)S(1)} %shard_map.120), channel_id=1, replica_groups=mesh['facet'=8,'sub'=32] {'sub'}, dimensions={0} | all-to-all | bytes 393216 | tf_op jit(solution)/shard_map/all_to_all | solution.py:454
  39.5 0.0 copy-done.6
  39.5 0.0 copy-done.9
  39.5 0.0 copy-done.10
  39.5 6.2 %shard_map.121 = bf16[32,8,128]{2,1,0:T(8,128)(2,1)S(1)} custom-call(bf16[32,24,128]{2,1,0:T(8,128)(2,1)S(1)} %all_to_all.15.arrived_ref, bf16[256,384]{1,0:T(8,128)(2,1)S(1)} %copy-done.6, bf16[128,128]{1,0:T(8,128)(2,1)S(1)} %copy-done.10, bf16[128,128]{1,0:T(8,128)(2,1)S(1)} %copy-done.9), custom_call_target="tpu_custom_call" | custom-call | flops 4294967296 | bytes 1048576 | tf_op jit(solution)/shard_map/pallas_call | solution.py:399
  45.7 11.9 %all_to_all.16.returned_ref = bf16[32,8,128]{2,1,0:T(8,128)(2,1)S(1)} all-to-all(bf16[32,8,128]{2,1,0:T(8,128)(2,1)S(1)} %shard_map.121), channel_id=1, replica_groups=mesh['facet'=8,'sub'=32] {'sub'}, dimensions={0} | all-to-all | bytes 131072 | tf_op jit(solution)/shard_map/all_to_all | solution.py:472
  57.7 1.5 %shard_map.122 = f32[2,4096]{1,0:T(2,128)} custom-call(bf16[32,8,128]{2,1,0:T(8,128)(2,1)S(1)} %all_to_all.16.returned_ref, s32[1,4096]{1,0:T(1,128)S(1)} %bitcast.3, s32[1,4096]{1,0:T(1,128)S(1)} %get-tuple-element.12.position_ref), custom_call_target="tpu_custom_call" | custom-call | flops 4294967296 | bytes 1048576 | tf_op jit(solution)/shard_map/pallas_call | solution.py:399
Async XLA Ops:
  0.0 0.8 %copy-start = (f32[1,2,2,2048]{3,2,1,0:T(2,128)S(1)}, f32[1,2,2,2048]{3,2,1,0:T(2,128)}, u32[]{:S(2)}) copy-start(f32[1,2,2,2048]{3,2,1,0:T(2,128)} %facets_ref.1) | copy-start | bytes 98308
  0.8 8.5 %copy-start.5 = (f32[256,2,256]{2,1,0:T(2,128)S(1)}, f32[256,2,256]{2,1,0:T(2,128)}, u32[]{:S(2)}) copy-start(f32[256,2,256]{2,1,0:T(2,128)} %constant.26.clone.inner_ref) | copy-start | bytes 1572868
  1.5 7.6 %copy-start.11 = (s32[256]{0:T(256)S(1)}, s32[256]{0:T(256)}, u32[]{:S(2)}) copy-start(s32[256]{0:T(256)} %param.14) | copy-start | bytes 3076
  1.5 7.7 %copy-start.1 = (f32[2,4096]{1,0:T(2,128)S(1)}, f32[2,4096]{1,0:T(2,128)}, u32[]{:S(2)}) copy-start(f32[2,4096]{1,0:T(2,128)} %coords_ref.1) | copy-start | bytes 98308
  1.5 15.2 %all-to-all-start = ((f32[8,64,128]{2,1,0:T(8,128)}), f32[8,64,128]{2,1,0:T(8,128)S(1)}, u32[]{:S(2)}, u32[]{:S(2)}) async-start(f32[8,64,128]{2,1,0:T(8,128)} %shard_map.118), calls=%async_computation | async-start | bytes 524288 | tf_op jit(solution)/shard_map/all_to_all | solution.py:420
  9.1 0.7 %copy-start.2 = (s32[4096,1]{0,1:T(1,128)S(1)}, s32[4096,1]{0,1:T(1,128)}, u32[]{:S(2)}) copy-start(s32[4096,1]{0,1:T(1,128)} %param.16) | copy-start | bytes 49156
  9.8 6.9 %copy-start.3 = (f32[2048]{0:T(1024)S(1)}, f32[2048]{0:T(1024)}, u32[]{:S(2)}) copy-start(f32[2048]{0:T(1024)} %param.13) | copy-start | bytes 24580
  9.8 6.9 %copy-start.4 = (f32[2,256,256]{2,1,0:T(8,128)S(1)}, f32[2,256,256]{2,1,0:T(8,128)}, u32[]{:S(2)}) copy-start(f32[2,256,256]{2,1,0:T(8,128)} %constant.29.clone.twiddle_ref) | copy-start | bytes 1572868
  9.8 6.9 %copy-start.7 = (bf16[128,512]{1,0:T(8,128)(2,1)S(1)}, bf16[128,512]{1,0:T(8,128)(2,1)}, u32[]{:S(2)}) copy-start(bf16[128,512]{1,0:T(8,128)(2,1)} %constant.28.clone.outer_l) | copy-start | bytes 393220
  9.8 6.9 %copy-start.8 = (bf16[128,512]{1,0:T(8,128)(2,1)S(1)}, bf16[128,512]{1,0:T(8,128)(2,1)}, u32[]{:S(2)}) copy-start(bf16[128,512]{1,0:T(8,128)(2,1)} %constant.27.clone.outer_h) | copy-start | bytes 393220
  18.5 21.1 %copy-start.6 = (bf16[256,384]{1,0:T(8,128)(2,1)S(1)}, bf16[256,384]{1,0:T(8,128)(2,1)}, u32[]{:S(2)}) copy-start(bf16[256,384]{1,0:T(8,128)(2,1)} %constant.30.clone.cells_ref) | copy-start | bytes 589828
  18.5 21.1 %copy-start.9 = (bf16[128,128]{1,0:T(8,128)(2,1)S(1)}, bf16[128,128]{1,0:T(8,128)(2,1)}, u32[]{:S(2)}) copy-start(bf16[128,128]{1,0:T(8,128)(2,1)} %constant.32.clone.with_sin_ref) | copy-start | bytes 98308
  18.5 21.0 %copy-start.10 = (bf16[128,128]{1,0:T(8,128)(2,1)S(1)}, bf16[128,128]{1,0:T(8,128)(2,1)}, u32[]{:S(2)}) copy-start(bf16[128,128]{1,0:T(8,128)(2,1)} %constant.31.clone.with_cos_ref) | copy-start | bytes 98308

commit v3 on v2

--- a/solution.py
+++ b/solution.py
@@ -113,7 +113,7 @@
 
 
 def pack_kernel(
-    starts_ref, coords_ref, owners_ref, inner_ref, packed_ref, position_ref, high_ref, low_ref, chosen
+    starts_ref, coords_ref, owners_ref, inner_ref, packed_ref, position_ref, slots_ref, high_ref, low_ref, chosen
 ):
     for s in range(SUBS):
         run = starts_ref[s] // 256
@@ -139,7 +139,10 @@
         rank = jnp.sum(hots[block] * (mine + carry), axis=0, keepdims=True) - 1.0
         carry = carry + mine[:, width - 1 : width]
         positions.append(rank.astype(jnp.int32))
-        position_ref[:, pl.ds(block * width, width)] = positions[-1]
+        lanes = pl.ds(block * width, width)
+        position_ref[:, lanes] = positions[-1]
+        own_slots = (iota((256, width), 0) == positions[-1] % 256).astype(F32)
+        slots_ref[:, lanes] = own_slots.astype(BF16)
     total = jnp.zeros((4 * SUBS, CAP), F32)
     for block in range(blocks):
         lanes = pl.ds(block * width, width)
@@ -361,7 +364,7 @@
     out_ref[...] = values[...].astype(BF16)
 
 
-def unpack_kernel(returned_ref, owners_ref, position_ref, out_ref, values):
+def unpack_kernel(returned_ref, owners_ref, position_ref, slots_ref, out_ref, values):
     values[...] = returned_ref[...].astype(F32)
     table = jnp.concatenate(
         [
@@ -372,15 +375,11 @@
     ).astype(BF16)
     width = 512
     owner_of = iota((2 * SUBS, width), 0) % SUBS
-    start_of = iota((2 * SUBS, width), 0) // SUBS * 256
-    slot_of = iota((256, width), 0)
+    late_of = iota((2 * SUBS, width), 0) // SUBS
     for block in range(DEV_ROWS // width):
         lanes = pl.ds(block * width, width)
-        position = position_ref[:, lanes]
-        late = position // 256 * 256
-        match = (owners_ref[:, lanes] == owner_of) & (late == start_of)
-        slots = (slot_of == position - late).astype(F32).astype(BF16)
-        picked = jnp.dot(table, slots, preferred_element_type=F32)
+        match = (owners_ref[:, lanes] == owner_of) & (position_ref[:, lanes] // 256 == late_of)
+        picked = jnp.dot(table, slots_ref[:, lanes], preferred_element_type=F32)
         for axis in range(2):
             out_ref[axis : axis + 1, lanes] = jnp.sum(
                 jnp.where(match, picked[64 * axis : 64 * axis + 64], 0.0), axis=0, keepdims=True
@@ -421,11 +420,12 @@
     owner_row = owners.reshape(1, DEV_ROWS)
     starts = lax.dynamic_slice(offsets, (facet_index * SUBS,), (SUBS,))
     inner, tables = transform_tables()
-    packed, position, chosen_h, chosen_l = call(
+    packed, position, slots, chosen_h, chosen_l = call(
         pack_kernel,
         (
             jax.ShapeDtypeStruct((SUBS, 16, 128), F32),
             jax.ShapeDtypeStruct((1, DEV_ROWS), jnp.int32),
+            jax.ShapeDtypeStruct((256, DEV_ROWS), BF16),
             jax.ShapeDtypeStruct((128, 256), BF16),
             jax.ShapeDtypeStruct((128, 256), BF16),
         ),
@@ -473,12 +473,13 @@
     return call(
         unpack_kernel,
         jax.ShapeDtypeStruct((2, DEV_ROWS), F32),
-        [vmem()] * 3,
+        [vmem()] * 4,
         [pltpu.VMEM((SUBS, 8, 128), F32)],
         1 << 32,
         returned,
         owner_row,
         position,
+        slots,
     )
 
 

time: 59.6 us -> 59.2 us (level)
  waiting for transfers between devices: 4.4 us -> 0.43 us
  local copies, waits for them, and re-layouts: 1.5 us -> 4.67 us
  Pallas kernels: 12.6 us -> 13.2 us
    all_to_all x1, waiting for transfers between devices: 4.4 us -> 0.43 us  [per_device(): lax.all_to_all(image, 'facet', split_axis=0, concat_axis=0, tiled=True)]
    unnamed x24 -> x28, local copies, waits for them, and re-layouts: 1.42 us -> 3.92 us
    dynamic_slice x1, local copies, waits for them, and re-layouts: 0.08 us -> 0.75 us  [per_device(): starts = lax.dynamic_slice(offsets, (facet_index * SUBS,), (SUBS,))]
  transfers between devices with their start and end apart: 1 -> 1, of which waited for: 1 -> 1; matrix products, arithmetic and copies ran while one was open for 0% -> 1% of each run, Pallas kernels for 4% -> 6%
where the time goes in v3:
time: 59.2 us; the launch traced here: 58.7 us
  blocking collectives  32.8 us (55%)
  Pallas kernels  13.2 us (22%)
  starting transfers between devices  7.48 us (13%)
  local copies, waits for them, and re-layouts  4.67 us (8%)
    all_to_all x1, blocking collectives, per_device(): lax.all_to_all(payload, 'sub', split_axis=0, concat_axis=0, tiled=True)  20.9 us
    pallas_call x5, Pallas kernels, call(): pl.pallas_call(kernel, out_shape=out_shape, in_specs=in_specs, out_specs=...  13.2 us
    all_to_all x1, blocking collectives, per_device(): lax.all_to_all(values, 'sub', split_axis=0, concat_axis=0, tiled=True)  11.9 us
    all_to_all x1, starting transfers between devices, per_device(): lax.all_to_all(image, 'facet', split_axis=0, concat_axis=0, tiled=True)  7.48 us
    unnamed x28, local copies, waits for them, and re-layouts  3.92 us
  transfers between devices with their start and end apart: 1, of which 1 were waited for; matrix products, arithmetic and copies ran while one was open for 1% of the time, Pallas kernels for 6%

profile of v3, /device:TPU:1, one launch (start us, length us, event | category | flops | bytes accessed | tf_op | source)
XLA Modules:
  0.0 58.7 jit_solution(13013495880157893477)
XLA Ops:
  0.0 0.0 copy-start
  0.0 0.8 %copy-done = f32[1,2,2,2048]{3,2,1,0:T(2,128)S(1)} copy-done((f32[1,2,2,2048]{3,2,1,0:T(2,128)S(1)}, f32[1,2,2,2048]{3,2,1,0:T(2,128)}, u32[]{:S(2)}) %copy-start) | copy-done | bytes 32792
  0.8 0.7 %shard_map.118 = f32[8,64,128]{2,1,0:T(8,128)} custom-call(f32[1,2,2,2048]{3,2,1,0:T(2,128)S(1)} %copy-done), custom_call_target="tpu_custom_call" | custom-call | bytes 1048576 | tf_op jit(solution)/shard_map/pallas_call | solution.py:398
  1.5 7.5 %all-to-all-start = ((f32[8,64,128]{2,1,0:T(8,128)}), f32[8,64,128]{2,1,0:T(8,128)S(1)}, u32[]{:S(2)}, u32[]{:S(2)}) async-start(f32[8,64,128]{2,1,0:T(8,128)} %shard_map.118), calls=%async_computation | async-start | bytes 524288 | tf_op jit(solution)/shard_map/all_to_all | solution.py:419
  9.0 0.8 %dynamic_slice.3.starts_ref = s32[32]{0:T(128)S(1)} dynamic-slice(s32[256]{0:T(256)} %param.14, s32[]{:T(128)S(6)} %select_n.3), dynamic_slice_sizes={32} | dynamic-slice | bytes 260 | tf_op jit(solution)/shard_map/dynamic_slice | solution.py:421
  9.7 0.0 copy-start.1
  9.7 0.8 %copy-done.1 = f32[2,4096]{1,0:T(2,128)S(1)} copy-done((f32[2,4096]{1,0:T(2,128)S(1)}, f32[2,4096]{1,0:T(2,128)}, u32[]{:S(2)}) %copy-start.1) | copy-done | bytes 32792
  10.5 0.0 copy-start.2
  10.5 0.7 %copy-done.2 = s32[4096,1]{0,1:T(1,128)S(1)} copy-done((s32[4096,1]{0,1:T(1,128)S(1)}, s32[4096,1]{0,1:T(1,128)}, u32[]{:S(2)}) %copy-start.2) | copy-done | bytes 16408
  11.2 0.0 copy-start.6
  11.2 1.0 %copy-done.6 = f32[256,2,256]{2,1,0:T(2,128)S(1)} copy-done((f32[256,2,256]{2,1,0:T(2,128)S(1)}, f32[256,2,256]{2,1,0:T(2,128)}, u32[]{:S(2)}) %copy-start.6) | copy-done | bytes 524312
  12.2 0.0 copy-start.4
  12.2 0.0 copy-start.5
  12.2 0.0 copy-start.8
  12.3 0.0 copy-start.9
  12.3 3.3 %shard_map.119 = (f32[32,16,128]{2,1,0:T(8,128)S(1)}, s32[1,4096]{1,0:T(1,128)S(1)}, bf16[256,4096]{1,0:T(8,128)(2,1)S(1)}, bf16[128,256]{1,0:T(8,128)(2,1)S(1)}, bf16[128,256]{1,0:T(8,128)(2,1)S(1)}) custom-call(s32[32]{0:T(128)S(1)} %dynamic_slice.3.starts_ref, f32[2,4096]{1,0:T(2,128)S(1)} %copy-done.1, s32[1,4096]{1,0:T(1,128)S(1)} %bitcast.2, ...), custom_call_target="tpu_custom_call" | custom-call | flops 4294967296 | bytes 1048576 | tf_op jit(solution)/shard_map/pallas_call | solution.py:398
  15.5 0.0 copy-start.12
  15.5 0.6 %copy-done.12 = s32[1,4096]{1,0:T(1,128)} copy-done((s32[1,4096]{1,0:T(1,128)}, s32[1,4096]{1,0:T(1,128)S(1)}, u32[]{:S(2)}) %copy-start.12) | copy-done | bytes 16408
  16.1 0.4 all-to-all-done.image_ref
  16.6 0.0 copy-done.4
  16.6 0.0 copy-done.5
  16.6 0.0 copy-done.8
  16.6 0.0 copy-done.9
  16.6 0.0 copy-start.7
  16.6 0.0 copy-start.10
  16.6 0.0 copy-start.11
  16.6 1.7 %shard_map.120 = bf16[32,24,128]{2,1,0:T(8,128)(2,1)S(1)} custom-call(s32[32]{0:T(128)S(1)} %dynamic_slice.3.starts_ref, f32[8,64,128]{2,1,0:T(8,128)S(1)} %all-to-all-done.image_ref, f32[16,128]{1,0:T(8,128)S(1)} %bitcast.4, f32[32,16,128]{2,1,0:T(8,128)S(1)} %get-tuple-element.10.packed_ref, bf16[128,256]{1,0:T(8,128)(2,1)S(1)} %get-tuple-element.11.chosen_h, ...), custom_call_target="tpu_custom_call" | custom-call | flops 4294967296 | bytes 1048576 | tf_op jit(solution)/shard_map/pallas_call | solution.py:398
  18.4 20.9 %all_to_all.15.arrived_ref = bf16[32,24,128]{2,1,0:T(8,128)(2,1)S(1)} all-to-all(bf16[32,24,128]{2,1,0:T(8,128)(2,1)S(1)} %shard_map.120), channel_id=1, replica_groups=mesh['facet'=8,'sub'=32] {'sub'}, dimensions={0} | all-to-all | bytes 393216 | tf_op jit(solution)/shard_map/all_to_all | solution.py:454
  39.2 0.0 copy-done.7
  39.2 0.0 copy-done.10
  39.2 0.0 copy-done.11
  39.3 0.0 copy-start.3
  39.3 0.0 copy-start.13
  39.3 6.2 %shard_map.121 = bf16[32,8,128]{2,1,0:T(8,128)(2,1)S(1)} custom-call(bf16[32,24,128]{2,1,0:T(8,128)(2,1)S(1)} %all_to_all.15.arrived_ref, bf16[256,384]{1,0:T(8,128)(2,1)S(1)} %copy-done.7, bf16[128,128]{1,0:T(8,128)(2,1)S(1)} %copy-done.11, bf16[128,128]{1,0:T(8,128)(2,1)S(1)} %copy-done.10), custom_call_target="tpu_custom_call" | custom-call | flops 4294967296 | bytes 1048576 | tf_op jit(solution)/shard_map/pallas_call | solution.py:398
  45.5 11.9 %all_to_all.16.returned_ref = bf16[32,8,128]{2,1,0:T(8,128)(2,1)S(1)} all-to-all(bf16[32,8,128]{2,1,0:T(8,128)(2,1)S(1)} %shard_map.121), channel_id=1, replica_groups=mesh['facet'=8,'sub'=32] {'sub'}, dimensions={0} | all-to-all | bytes 131072 | tf_op jit(solution)/shard_map/all_to_all | solution.py:472
  57.5 0.0 copy-done.3
  57.5 0.0 copy-done.13
  57.5 1.2 %shard_map.122 = f32[2,4096]{1,0:T(2,128)} custom-call(bf16[32,8,128]{2,1,0:T(8,128)(2,1)S(1)} %all_to_all.16.returned_ref, s32[1,4096]{1,0:T(1,128)S(1)} %bitcast.3, s32[1,4096]{1,0:T(1,128)S(1)} %copy-done.13, bf16[256,4096]{1,0:T(8,128)(2,1)S(1)} %get-tuple-element.14.slots_ref), custom_call_target="tpu_custom_call" | custom-call | flops 4294967296 | bytes 1048576 | tf_op jit(solution)/shard_map/pallas_call | solution.py:398
Async XLA Ops:
  0.0 0.8 %copy-start = (f32[1,2,2,2048]{3,2,1,0:T(2,128)S(1)}, f32[1,2,2,2048]{3,2,1,0:T(2,128)}, u32[]{:S(2)}) copy-start(f32[1,2,2,2048]{3,2,1,0:T(2,128)} %facets_ref.1) | copy-start | bytes 98308
  1.5 15.1 %all-to-all-start = ((f32[8,64,128]{2,1,0:T(8,128)}), f32[8,64,128]{2,1,0:T(8,128)S(1)}, u32[]{:S(2)}, u32[]{:S(2)}) async-start(f32[8,64,128]{2,1,0:T(8,128)} %shard_map.118), calls=%async_computation | async-start | bytes 524288 | tf_op jit(solution)/shard_map/all_to_all | solution.py:419
  9.7 0.8 %copy-start.1 = (f32[2,4096]{1,0:T(2,128)S(1)}, f32[2,4096]{1,0:T(2,128)}, u32[]{:S(2)}) copy-start(f32[2,4096]{1,0:T(2,128)} %coords_ref.1) | copy-start | bytes 98308
  10.5 0.7 %copy-start.2 = (s32[4096,1]{0,1:T(1,128)S(1)}, s32[4096,1]{0,1:T(1,128)}, u32[]{:S(2)}) copy-start(s32[4096,1]{0,1:T(1,128)} %param.16) | copy-start | bytes 49156
  11.2 1.0 %copy-start.6 = (f32[256,2,256]{2,1,0:T(2,128)S(1)}, f32[256,2,256]{2,1,0:T(2,128)}, u32[]{:S(2)}) copy-start(f32[256,2,256]{2,1,0:T(2,128)} %constant.26.clone.inner_ref) | copy-start | bytes 1572868
  12.2 4.3 %copy-start.4 = (f32[2048]{0:T(1024)S(1)}, f32[2048]{0:T(1024)}, u32[]{:S(2)}) copy-start(f32[2048]{0:T(1024)} %param.13) | copy-start | bytes 24580
  12.2 4.3 %copy-start.5 = (f32[2,256,256]{2,1,0:T(8,128)S(1)}, f32[2,256,256]{2,1,0:T(8,128)}, u32[]{:S(2)}) copy-start(f32[2,256,256]{2,1,0:T(8,128)} %constant.29.clone.twiddle_ref) | copy-start | bytes 1572868
  12.2 4.3 %copy-start.8 = (bf16[128,512]{1,0:T(8,128)(2,1)S(1)}, bf16[128,512]{1,0:T(8,128)(2,1)}, u32[]{:S(2)}) copy-start(bf16[128,512]{1,0:T(8,128)(2,1)} %constant.28.clone.outer_l) | copy-start | bytes 393220
  12.3 4.3 %copy-start.9 = (bf16[128,512]{1,0:T(8,128)(2,1)S(1)}, bf16[128,512]{1,0:T(8,128)(2,1)}, u32[]{:S(2)}) copy-start(bf16[128,512]{1,0:T(8,128)(2,1)} %constant.27.clone.outer_h) | copy-start | bytes 393220
  15.5 0.6 %copy-start.12 = (s32[1,4096]{1,0:T(1,128)}, s32[1,4096]{1,0:T(1,128)S(1)}, u32[]{:S(2)}) copy-start(s32[1,4096]{1,0:T(1,128)S(1)} %get-tuple-element.13.position_ref) | copy-start | bytes 49156
  16.6 22.7 %copy-start.7 = (bf16[256,384]{1,0:T(8,128)(2,1)S(1)}, bf16[256,384]{1,0:T(8,128)(2,1)}, u32[]{:S(2)}) copy-start(bf16[256,384]{1,0:T(8,128)(2,1)} %constant.30.clone.cells_ref) | copy-start | bytes 589828
  16.6 22.7 %copy-start.10 = (bf16[128,128]{1,0:T(8,128)(2,1)S(1)}, bf16[128,128]{1,0:T(8,128)(2,1)}, u32[]{:S(2)}) copy-start(bf16[128,128]{1,0:T(8,128)(2,1)} %constant.32.clone.with_sin_ref) | copy-start | bytes 98308
  16.6 22.6 %copy-start.11 = (bf16[128,128]{1,0:T(8,128)(2,1)S(1)}, bf16[128,128]{1,0:T(8,128)(2,1)}, u32[]{:S(2)}) copy-start(bf16[128,128]{1,0:T(8,128)(2,1)} %constant.31.clone.with_cos_ref) | copy-start | bytes 98308
  39.3 18.2 %copy-start.3 = (s32[4096,1]{0,1:T(1,128)S(1)}, s32[4096,1]{0,1:T(1,128)}, u32[]{:S(2)}) copy-start(s32[4096,1]{0,1:T(1,128)} %param.16) | copy-start | bytes 49156
  39.3 18.2 %copy-start.13 = (s32[1,4096]{1,0:T(1,128)S(1)}, s32[1,4096]{1,0:T(1,128)}, u32[]{:S(2)}) copy-start(s32[1,4096]{1,0:T(1,128)} %copy-done.12) | copy-start | bytes 49156

commit v4 on v3

--- a/solution.py
+++ b/solution.py
@@ -15,7 +15,7 @@
 SUBS = 32
 CAP = 512
 DEV_ROWS = 4096
-PARTS = 4
+PARTS = 8
 F32 = jnp.float32
 BF16 = jnp.bfloat16
 
@@ -231,7 +231,7 @@
 
 
 def degrid_kernel(
-    arrived_ref, cells_ref, with_cos_ref, with_sin_ref, out_ref, arrived, coords, weights, bias, partial, values, *buffers
+    arrived_ref, cells_ref, with_cos_ref, with_sin_ref, out_ref, arrived, coords, weights, bias, partial, values, phases
 ):
     arrived[...] = arrived_ref[...].astype(F32)
     grid = jnp.concatenate(
@@ -326,29 +326,24 @@
         for number, piece in enumerate(made):
             buffer[16 * number : 16 * number + 16, :] = piece
 
-    def turn(step, ready, following):
-        later = jnp.minimum(step + 1, steps - 1)
-        inners = [
-            jnp.dot(weights[...], ready[part][...], preferred_element_type=F32)
-            for part in range(PARTS)
-        ]
-        made = [make_phases(later, part) for part in range(PARTS)]
-        sums = [evaluate(step, part, inners[part]) for part in range(PARTS)]
+    def produce(step, carry):
         for part in range(PARTS):
-            fill(made[part], following[part])
-            source, half = place(step, part)
+            fill(make_phases(step, part), phases.at[step * PARTS + part])
+        return carry
+
+    def consume(step, carry):
+        for part in range(2 * PARTS):
+            inner = jnp.dot(
+                weights[...], phases[step * 2 * PARTS + part], preferred_element_type=F32
+            )
+            sums = evaluate(2 * step, part, inner)
+            source, half = place(2 * step, part)
             for axis in range(2):
-                partial[axis, half, source] = sums[part][axis]
-
-    def both(pair, carry):
-        turn(2 * pair, first, second)
-        turn(2 * pair + 1, second, first)
+                partial[axis, half, source] = sums[axis]
         return carry
 
-    first, second = buffers[:PARTS], buffers[PARTS:]
-    for part in range(PARTS):
-        fill(make_phases(0, part), first[part])
-    lax.fori_loop(0, steps // 2, both, 0)
+    lax.fori_loop(0, steps, produce, 0)
+    lax.fori_loop(0, steps // 2, consume, 0)
     for half in range(2):
         where = jnp.concatenate([coords[0, 2 * half], coords[0, 2 * half + 1]], axis=1)
         back_cos, back_sin = unit_turns(where * (0.5 / ROWS), QUARTER_TURN)
@@ -463,8 +458,8 @@
             pltpu.VMEM((128, 128), F32),
             pltpu.VMEM((2, 2, SUBS, 8, 256), F32),
             pltpu.VMEM((SUBS, 8, 128), F32),
-        ]
-        + [pltpu.VMEM((256, 256), BF16)] * (2 * PARTS),
+            pltpu.VMEM((2 * SUBS, 256, 256), BF16),
+        ],
         1 << 32,
         arrived,
         *fold_tables(),

time: 59.2 us -> 58.9 us (level)
  no operation moved by 1% of the time
where the time goes in v4:
time: 58.9 us; the launch traced here: 58.4 us
  blocking collectives  32.8 us (56%)
  Pallas kernels  12.9 us (22%)
  starting transfers between devices  7.48 us (13%)
  local copies, waits for them, and re-layouts  4.67 us (8%)
    all_to_all x1, blocking collectives, per_device(): lax.all_to_all(payload, 'sub', split_axis=0, concat_axis=0, tiled=True)  20.9 us
    pallas_call x5, Pallas kernels, call(): pl.pallas_call(kernel, out_shape=out_shape, in_specs=in_specs, out_specs=...  12.9 us
    all_to_all x1, blocking collectives, per_device(): lax.all_to_all(values, 'sub', split_axis=0, concat_axis=0, tiled=True)  11.9 us
    all_to_all x1, starting transfers between devices, per_device(): lax.all_to_all(image, 'facet', split_axis=0, concat_axis=0, tiled=True)  7.48 us
    unnamed x28, local copies, waits for them, and re-layouts  3.92 us
  transfers between devices with their start and end apart: 1, of which 1 were waited for; matrix products, arithmetic and copies ran while one was open for 1% of the time, Pallas kernels for 6%

profile of v4, /device:TPU:1, one launch (start us, length us, event | category | flops | bytes accessed | tf_op | source)
XLA Modules:
  0.0 58.4 jit_solution(10081901932187078580)
XLA Ops:
  0.0 0.0 copy-start
  0.0 0.8 %copy-done = f32[1,2,2,2048]{3,2,1,0:T(2,128)S(1)} copy-done((f32[1,2,2,2048]{3,2,1,0:T(2,128)S(1)}, f32[1,2,2,2048]{3,2,1,0:T(2,128)}, u32[]{:S(2)}) %copy-start) | copy-done | bytes 32792
  0.8 0.7 %shard_map.118 = f32[8,64,128]{2,1,0:T(8,128)} custom-call(f32[1,2,2,2048]{3,2,1,0:T(2,128)S(1)} %copy-done), custom_call_target="tpu_custom_call" | custom-call | bytes 1048576 | tf_op jit(solution)/shard_map/pallas_call | solution.py:393
  1.5 7.5 %all-to-all-start = ((f32[8,64,128]{2,1,0:T(8,128)}), f32[8,64,128]{2,1,0:T(8,128)S(1)}, u32[]{:S(2)}, u32[]{:S(2)}) async-start(f32[8,64,128]{2,1,0:T(8,128)} %shard_map.118), calls=%async_computation | async-start | bytes 524288 | tf_op jit(solution)/shard_map/all_to_all | solution.py:414
  9.0 0.8 %dynamic_slice.3.starts_ref = s32[32]{0:T(128)S(1)} dynamic-slice(s32[256]{0:T(256)} %param.14, s32[]{:T(128)S(6)} %select_n.3), dynamic_slice_sizes={32} | dynamic-slice | bytes 260 | tf_op jit(solution)/shard_map/dynamic_slice | solution.py:416
  9.7 0.0 copy-start.1
  9.7 0.8 %copy-done.1 = f32[2,4096]{1,0:T(2,128)S(1)} copy-done((f32[2,4096]{1,0:T(2,128)S(1)}, f32[2,4096]{1,0:T(2,128)}, u32[]{:S(2)}) %copy-start.1) | copy-done | bytes 32792
  10.5 0.0 copy-start.2
  10.5 0.7 %copy-done.2 = s32[4096,1]{0,1:T(1,128)S(1)} copy-done((s32[4096,1]{0,1:T(1,128)S(1)}, s32[4096,1]{0,1:T(1,128)}, u32[]{:S(2)}) %copy-start.2) | copy-done | bytes 16408
  11.2 0.0 copy-start.6
  11.2 1.0 %copy-done.6 = f32[256,2,256]{2,1,0:T(2,128)S(1)} copy-done((f32[256,2,256]{2,1,0:T(2,128)S(1)}, f32[256,2,256]{2,1,0:T(2,128)}, u32[]{:S(2)}) %copy-start.6) | copy-done | bytes 524312
  12.2 0.0 copy-start.4
  12.2 0.0 copy-start.5
  12.2 0.0 copy-start.8
  12.3 0.0 copy-start.9
  12.3 3.3 %shard_map.119 = (f32[32,16,128]{2,1,0:T(8,128)S(1)}, s32[1,4096]{1,0:T(1,128)S(1)}, bf16[256,4096]{1,0:T(8,128)(2,1)S(1)}, bf16[128,256]{1,0:T(8,128)(2,1)S(1)}, bf16[128,256]{1,0:T(8,128)(2,1)S(1)}) custom-call(s32[32]{0:T(128)S(1)} %dynamic_slice.3.starts_ref, f32[2,4096]{1,0:T(2,128)S(1)} %copy-done.1, s32[1,4096]{1,0:T(1,128)S(1)} %bitcast.2, ...), custom_call_target="tpu_custom_call" | custom-call | flops 4294967296 | bytes 1048576 | tf_op jit(solution)/shard_map/pallas_call | solution.py:393
  15.5 0.0 copy-start.12
  15.5 0.6 %copy-done.12 = s32[1,4096]{1,0:T(1,128)} copy-done((s32[1,4096]{1,0:T(1,128)}, s32[1,4096]{1,0:T(1,128)S(1)}, u32[]{:S(2)}) %copy-start.12) | copy-done | bytes 16408
  16.1 0.4 all-to-all-done.image_ref
  16.6 0.0 copy-done.4
  16.6 0.0 copy-done.5
  16.6 0.0 copy-done.8
  16.6 0.0 copy-done.9
  16.6 0.0 copy-start.7
  16.6 0.0 copy-start.10
  16.6 0.0 copy-start.11
  16.6 1.7 %shard_map.120 = bf16[32,24,128]{2,1,0:T(8,128)(2,1)S(1)} custom-call(s32[32]{0:T(128)S(1)} %dynamic_slice.3.starts_ref, f32[8,64,128]{2,1,0:T(8,128)S(1)} %all-to-all-done.image_ref, f32[16,128]{1,0:T(8,128)S(1)} %bitcast.4, f32[32,16,128]{2,1,0:T(8,128)S(1)} %get-tuple-element.10.packed_ref, bf16[128,256]{1,0:T(8,128)(2,1)S(1)} %get-tuple-element.11.chosen_h, ...), custom_call_target="tpu_custom_call" | custom-call | flops 4294967296 | bytes 1048576 | tf_op jit(solution)/shard_map/pallas_call | solution.py:393
  18.4 20.9 %all_to_all.15.arrived_ref = bf16[32,24,128]{2,1,0:T(8,128)(2,1)S(1)} all-to-all(bf16[32,24,128]{2,1,0:T(8,128)(2,1)S(1)} %shard_map.120), channel_id=1, replica_groups=mesh['facet'=8,'sub'=32] {'sub'}, dimensions={0} | all-to-all | bytes 393216 | tf_op jit(solution)/shard_map/all_to_all | solution.py:449
  39.2 0.0 copy-done.7
  39.2 0.0 copy-done.10
  39.2 0.0 copy-done.11
  39.3 0.0 copy-start.3
  39.3 0.0 copy-start.13
  39.3 5.9 %shard_map.121 = bf16[32,8,128]{2,1,0:T(8,128)(2,1)S(1)} custom-call(bf16[32,24,128]{2,1,0:T(8,128)(2,1)S(1)} %all_to_all.15.arrived_ref, bf16[256,384]{1,0:T(8,128)(2,1)S(1)} %copy-done.7, bf16[128,128]{1,0:T(8,128)(2,1)S(1)} %copy-done.11, bf16[128,128]{1,0:T(8,128)(2,1)S(1)} %copy-done.10), custom_call_target="tpu_custom_call" | custom-call | flops 4294967296 | bytes 1048576 | tf_op jit(solution)/shard_map/pallas_call | solution.py:393
  45.2 11.9 %all_to_all.16.returned_ref = bf16[32,8,128]{2,1,0:T(8,128)(2,1)S(1)} all-to-all(bf16[32,8,128]{2,1,0:T(8,128)(2,1)S(1)} %shard_map.121), channel_id=1, replica_groups=mesh['facet'=8,'sub'=32] {'sub'}, dimensions={0} | all-to-all | bytes 131072 | tf_op jit(solution)/shard_map/all_to_all | solution.py:467
  57.2 0.0 copy-done.3
  57.2 0.0 copy-done.13
  57.2 1.2 %shard_map.122 = f32[2,4096]{1,0:T(2,128)} custom-call(bf16[32,8,128]{2,1,0:T(8,128)(2,1)S(1)} %all_to_all.16.returned_ref, s32[1,4096]{1,0:T(1,128)S(1)} %bitcast.3, s32[1,4096]{1,0:T(1,128)S(1)} %copy-done.13, bf16[256,4096]{1,0:T(8,128)(2,1)S(1)} %get-tuple-element.14.slots_ref), custom_call_target="tpu_custom_call" | custom-call | flops 4294967296 | bytes 1048576 | tf_op jit(solution)/shard_map/pallas_call | solution.py:393
Async XLA Ops:
  0.0 0.8 %copy-start = (f32[1,2,2,2048]{3,2,1,0:T(2,128)S(1)}, f32[1,2,2,2048]{3,2,1,0:T(2,128)}, u32[]{:S(2)}) copy-start(f32[1,2,2,2048]{3,2,1,0:T(2,128)} %facets_ref.1) | copy-start | bytes 98308
  1.5 15.1 %all-to-all-start = ((f32[8,64,128]{2,1,0:T(8,128)}), f32[8,64,128]{2,1,0:T(8,128)S(1)}, u32[]{:S(2)}, u32[]{:S(2)}) async-start(f32[8,64,128]{2,1,0:T(8,128)} %shard_map.118), calls=%async_computation | async-start | bytes 524288 | tf_op jit(solution)/shard_map/all_to_all | solution.py:414
  9.7 0.8 %copy-start.1 = (f32[2,4096]{1,0:T(2,128)S(1)}, f32[2,4096]{1,0:T(2,128)}, u32[]{:S(2)}) copy-start(f32[2,4096]{1,0:T(2,128)} %coords_ref.1) | copy-start | bytes 98308
  10.5 0.7 %copy-start.2 = (s32[4096,1]{0,1:T(1,128)S(1)}, s32[4096,1]{0,1:T(1,128)}, u32[]{:S(2)}) copy-start(s32[4096,1]{0,1:T(1,128)} %param.16) | copy-start | bytes 49156
  11.2 1.0 %copy-start.6 = (f32[256,2,256]{2,1,0:T(2,128)S(1)}, f32[256,2,256]{2,1,0:T(2,128)}, u32[]{:S(2)}) copy-start(f32[256,2,256]{2,1,0:T(2,128)} %constant.26.clone.inner_ref) | copy-start | bytes 1572868
  12.2 4.3 %copy-start.4 = (f32[2048]{0:T(1024)S(1)}, f32[2048]{0:T(1024)}, u32[]{:S(2)}) copy-start(f32[2048]{0:T(1024)} %param.13) | copy-start | bytes 24580
  12.2 4.3 %copy-start.5 = (f32[2,256,256]{2,1,0:T(8,128)S(1)}, f32[2,256,256]{2,1,0:T(8,128)}, u32[]{:S(2)}) copy-start(f32[2,256,256]{2,1,0:T(8,128)} %constant.29.clone.twiddle_ref) | copy-start | bytes 1572868
  12.2 4.3 %copy-start.8 = (bf16[128,512]{1,0:T(8,128)(2,1)S(1)}, bf16[128,512]{1,0:T(8,128)(2,1)}, u32[]{:S(2)}) copy-start(bf16[128,512]{1,0:T(8,128)(2,1)} %constant.28.clone.outer_l) | copy-start | bytes 393220
  12.3 4.3 %copy-start.9 = (bf16[128,512]{1,0:T(8,128)(2,1)S(1)}, bf16[128,512]{1,0:T(8,128)(2,1)}, u32[]{:S(2)}) copy-start(bf16[128,512]{1,0:T(8,128)(2,1)} %constant.27.clone.outer_h) | copy-start | bytes 393220
  15.5 0.6 %copy-start.12 = (s32[1,4096]{1,0:T(1,128)}, s32[1,4096]{1,0:T(1,128)S(1)}, u32[]{:S(2)}) copy-start(s32[1,4096]{1,0:T(1,128)S(1)} %get-tuple-element.13.position_ref) | copy-start | bytes 49156
  16.6 22.7 %copy-start.7 = (bf16[256,384]{1,0:T(8,128)(2,1)S(1)}, bf16[256,384]{1,0:T(8,128)(2,1)}, u32[]{:S(2)}) copy-start(bf16[256,384]{1,0:T(8,128)(2,1)} %constant.30.clone.cells_ref) | copy-start | bytes 589828
  16.6 22.7 %copy-start.10 = (bf16[128,128]{1,0:T(8,128)(2,1)S(1)}, bf16[128,128]{1,0:T(8,128)(2,1)}, u32[]{:S(2)}) copy-start(bf16[128,128]{1,0:T(8,128)(2,1)} %constant.32.clone.with_sin_ref) | copy-start | bytes 98308
  16.6 22.6 %copy-start.11 = (bf16[128,128]{1,0:T(8,128)(2,1)S(1)}, bf16[128,128]{1,0:T(8,128)(2,1)}, u32[]{:S(2)}) copy-start(bf16[128,128]{1,0:T(8,128)(2,1)} %constant.31.clone.with_cos_ref) | copy-start | bytes 98308
  39.3 17.9 %copy-start.3 = (s32[4096,1]{0,1:T(1,128)S(1)}, s32[4096,1]{0,1:T(1,128)}, u32[]{:S(2)}) copy-start(s32[4096,1]{0,1:T(1,128)} %param.16) | copy-start | bytes 49156
  39.3 17.9 %copy-start.13 = (s32[1,4096]{1,0:T(1,128)S(1)}, s32[1,4096]{1,0:T(1,128)}, u32[]{:S(2)}) copy-start(s32[1,4096]{1,0:T(1,128)} %copy-done.12) | copy-start | bytes 49156

commit v5 on v4

--- a/solution.py
+++ b/solution.py
@@ -15,7 +15,7 @@
 SUBS = 32
 CAP = 512
 DEV_ROWS = 4096
-PARTS = 8
+PARTS = 16
 F32 = jnp.float32
 BF16 = jnp.bfloat16
 
@@ -78,7 +78,7 @@
 
 ANY_TURN = turn_polynomials(0.5, 7, 6)
 QUARTER_TURN = turn_polynomials(0.25, 5, 5)
-SMALL_TURN = turn_polynomials(0.0625, 4, 3)
+SMALL_TURN = turn_polynomials(0.125, 4, 4)
 
 
 def reduced(turns):
@@ -258,34 +258,29 @@
     bias[...] = fold(with_cos_ref[...], slice(256, 384))
 
     step_row = iota((8, 256), 0).astype(F32)
-    cell_scale = (16.0 * step_row + 8.5) * (1.0 / XA)
+    cell_scale = (16.0 * step_row + 8.0) * (1.0 / XA)
     row_scale = (4.0 * step_row + 2.0) * (1.0 / ROWS)
     def place(step, part):
         return (step * PARTS + part) // 2, part % 2
 
-    def beside(step, part, axis):
+    def seeds(step, part, axis, scale):
         source, half = place(step, part)
         where = jnp.concatenate(
             [
                 jnp.broadcast_to(
-                    coords[1 - axis, 2 * half + side, pl.ds(source, 1), :], (8, 128)
+                    coords[axis, 2 * half + side, pl.ds(source, 1), :], (8, 128)
                 )
                 for side in range(2)
             ],
             axis=1,
         )
-        scale, terms, centre_scale = (
-            (0.5 / XA, SMALL_TURN, cell_scale),
-            (0.5 / ROWS, QUARTER_TURN, row_scale),
-        )[axis]
-        a_cos, a_sin = unit_turns(reduced(where * centre_scale), ANY_TURN)
-        b_cos, b_sin = unit_turns(where * scale, terms)
-        cc, ss = a_cos * b_cos, a_sin * b_sin
-        sc, cs = a_sin * b_cos, a_cos * b_sin
-        return (cc + ss, sc - cs), (cc - ss, sc + cs), double_cos((b_cos, b_sin))
+        return where, unit_turns(reduced(where * scale), ANY_TURN)
 
     def make_phases(step, part):
-        below, above, twice = beside(step, part, 0)
+        u, below = seeds(step, part, 1, cell_scale)
+        (a_cos, a_sin), (b_cos, b_sin) = below, unit_turns(u * (1.0 / XA), SMALL_TURN)
+        above = (a_cos * b_cos - a_sin * b_sin, a_sin * b_cos + a_cos * b_sin)
+        twice = b_cos + b_cos
         pieces = [[None] * 8, [None] * 8]
         for direction in (-1, 1):
             last, before, at = (below, above, 3) if direction < 0 else (above, below, 4)
@@ -303,7 +298,12 @@
         return pieces[0] + pieces[1]
 
     def evaluate(step, part, inner):
-        below, above, twice = beside(step, part, 1)
+        v, (a_cos, a_sin) = seeds(step, part, 0, row_scale)
+        half_step = unit_turns(v * (0.5 / ROWS), QUARTER_TURN)
+        b_cos, b_sin = half_step
+        cc, ss = a_cos * b_cos, a_sin * b_sin
+        sc, cs = a_sin * b_cos, a_cos * b_sin
+        below, above, twice = (cc + ss, sc - cs), (cc - ss, sc + cs), double_cos(half_step)
         total_real = total_imag = 0.0
         for j in (1, 0, 2, 3):
             if j == 0:

time: 58.9 us -> 58.7 us (level)
  no operation moved by 1% of the time
where the time goes in v5:
time: 58.7 us; the launch traced here: 58.2 us
  blocking collectives  32.8 us (56%)
  Pallas kernels  12.7 us (22%)
  starting transfers between devices  7.48 us (13%)
  local copies, waits for them, and re-layouts  4.67 us (8%)
    all_to_all x1, blocking collectives, per_device(): lax.all_to_all(payload, 'sub', split_axis=0, concat_axis=0, tiled=True)  20.9 us
    pallas_call x5, Pallas kernels, call(): pl.pallas_call(kernel, out_shape=out_shape, in_specs=in_specs, out_specs=...  12.7 us
    all_to_all x1, blocking collectives, per_device(): lax.all_to_all(values, 'sub', split_axis=0, concat_axis=0, tiled=True)  11.9 us
    all_to_all x1, starting transfers between devices, per_device(): lax.all_to_all(image, 'facet', split_axis=0, concat_axis=0, tiled=True)  7.48 us
    unnamed x28, local copies, waits for them, and re-layouts  3.92 us
  transfers between devices with their start and end apart: 1, of which 1 were waited for; matrix products, arithmetic and copies ran while one was open for 1% of the time, Pallas kernels for 6%

profile of v5, /device:TPU:1, one launch (start us, length us, event | category | flops | bytes accessed | tf_op | source)
XLA Modules:
  0.0 58.2 jit_solution(4669184374507755697)
XLA Ops:
  0.0 0.0 copy-start
  0.0 0.8 %copy-done = f32[1,2,2,2048]{3,2,1,0:T(2,128)S(1)} copy-done((f32[1,2,2,2048]{3,2,1,0:T(2,128)S(1)}, f32[1,2,2,2048]{3,2,1,0:T(2,128)}, u32[]{:S(2)}) %copy-start) | copy-done | bytes 32792
  0.8 0.7 %shard_map.118 = f32[8,64,128]{2,1,0:T(8,128)} custom-call(f32[1,2,2,2048]{3,2,1,0:T(2,128)S(1)} %copy-done), custom_call_target="tpu_custom_call" | custom-call | bytes 1048576 | tf_op jit(solution)/shard_map/pallas_call | solution.py:393
  1.5 7.5 %all-to-all-start = ((f32[8,64,128]{2,1,0:T(8,128)}), f32[8,64,128]{2,1,0:T(8,128)S(1)}, u32[]{:S(2)}, u32[]{:S(2)}) async-start(f32[8,64,128]{2,1,0:T(8,128)} %shard_map.118), calls=%async_computation | async-start | bytes 524288 | tf_op jit(solution)/shard_map/all_to_all | solution.py:414
  9.0 0.8 %dynamic_slice.3.starts_ref = s32[32]{0:T(128)S(1)} dynamic-slice(s32[256]{0:T(256)} %param.14, s32[]{:T(128)S(6)} %select_n.3), dynamic_slice_sizes={32} | dynamic-slice | bytes 260 | tf_op jit(solution)/shard_map/dynamic_slice | solution.py:416
  9.7 0.0 copy-start.1
  9.7 0.8 %copy-done.1 = f32[2,4096]{1,0:T(2,128)S(1)} copy-done((f32[2,4096]{1,0:T(2,128)S(1)}, f32[2,4096]{1,0:T(2,128)}, u32[]{:S(2)}) %copy-start.1) | copy-done | bytes 32792
  10.5 0.0 copy-start.2
  10.5 0.7 %copy-done.2 = s32[4096,1]{0,1:T(1,128)S(1)} copy-done((s32[4096,1]{0,1:T(1,128)S(1)}, s32[4096,1]{0,1:T(1,128)}, u32[]{:S(2)}) %copy-start.2) | copy-done | bytes 16408
  11.2 0.0 copy-start.6
  11.2 1.0 %copy-done.6 = f32[256,2,256]{2,1,0:T(2,128)S(1)} copy-done((f32[256,2,256]{2,1,0:T(2,128)S(1)}, f32[256,2,256]{2,1,0:T(2,128)}, u32[]{:S(2)}) %copy-start.6) | copy-done | bytes 524312
  12.2 0.0 copy-start.4
  12.2 0.0 copy-start.5
  12.2 0.0 copy-start.8
  12.3 0.0 copy-start.9
  12.3 3.3 %shard_map.119 = (f32[32,16,128]{2,1,0:T(8,128)S(1)}, s32[1,4096]{1,0:T(1,128)S(1)}, bf16[256,4096]{1,0:T(8,128)(2,1)S(1)}, bf16[128,256]{1,0:T(8,128)(2,1)S(1)}, bf16[128,256]{1,0:T(8,128)(2,1)S(1)}) custom-call(s32[32]{0:T(128)S(1)} %dynamic_slice.3.starts_ref, f32[2,4096]{1,0:T(2,128)S(1)} %copy-done.1, s32[1,4096]{1,0:T(1,128)S(1)} %bitcast.2, ...), custom_call_target="tpu_custom_call" | custom-call | flops 4294967296 | bytes 1048576 | tf_op jit(solution)/shard_map/pallas_call | solution.py:393
  15.5 0.0 copy-start.12
  15.5 0.6 %copy-done.12 = s32[1,4096]{1,0:T(1,128)} copy-done((s32[1,4096]{1,0:T(1,128)}, s32[1,4096]{1,0:T(1,128)S(1)}, u32[]{:S(2)}) %copy-start.12) | copy-done | bytes 16408
  16.1 0.4 all-to-all-done.image_ref
  16.6 0.0 copy-done.4
  16.6 0.0 copy-done.5
  16.6 0.0 copy-done.8
  16.6 0.0 copy-done.9
  16.6 0.0 copy-start.7
  16.6 0.0 copy-start.10
  16.6 0.0 copy-start.11
  16.6 1.7 %shard_map.120 = bf16[32,24,128]{2,1,0:T(8,128)(2,1)S(1)} custom-call(s32[32]{0:T(128)S(1)} %dynamic_slice.3.starts_ref, f32[8,64,128]{2,1,0:T(8,128)S(1)} %all-to-all-done.image_ref, f32[16,128]{1,0:T(8,128)S(1)} %bitcast.4, f32[32,16,128]{2,1,0:T(8,128)S(1)} %get-tuple-element.10.packed_ref, bf16[128,256]{1,0:T(8,128)(2,1)S(1)} %get-tuple-element.11.chosen_h, ...), custom_call_target="tpu_custom_call" | custom-call | flops 4294967296 | bytes 1048576 | tf_op jit(solution)/shard_map/pallas_call | solution.py:393
  18.4 20.9 %all_to_all.15.arrived_ref = bf16[32,24,128]{2,1,0:T(8,128)(2,1)S(1)} all-to-all(bf16[32,24,128]{2,1,0:T(8,128)(2,1)S(1)} %shard_map.120), channel_id=1, replica_groups=mesh['facet'=8,'sub'=32] {'sub'}, dimensions={0} | all-to-all | bytes 393216 | tf_op jit(solution)/shard_map/all_to_all | solution.py:449
  39.2 0.0 copy-done.7
  39.2 0.0 copy-done.10
  39.2 0.0 copy-done.11
  39.3 0.0 copy-start.3
  39.3 0.0 copy-start.13
  39.3 5.8 %shard_map.121 = bf16[32,8,128]{2,1,0:T(8,128)(2,1)S(1)} custom-call(bf16[32,24,128]{2,1,0:T(8,128)(2,1)S(1)} %all_to_all.15.arrived_ref, bf16[256,384]{1,0:T(8,128)(2,1)S(1)} %copy-done.7, bf16[128,128]{1,0:T(8,128)(2,1)S(1)} %copy-done.11, bf16[128,128]{1,0:T(8,128)(2,1)S(1)} %copy-done.10), custom_call_target="tpu_custom_call" | custom-call | flops 4294967296 | bytes 1048576 | tf_op jit(solution)/shard_map/pallas_call | solution.py:393
  45.0 11.9 %all_to_all.16.returned_ref = bf16[32,8,128]{2,1,0:T(8,128)(2,1)S(1)} all-to-all(bf16[32,8,128]{2,1,0:T(8,128)(2,1)S(1)} %shard_map.121), channel_id=1, replica_groups=mesh['facet'=8,'sub'=32] {'sub'}, dimensions={0} | all-to-all | bytes 131072 | tf_op jit(solution)/shard_map/all_to_all | solution.py:467
  57.0 0.0 copy-done.3
  57.0 0.0 copy-done.13
  57.0 1.2 %shard_map.122 = f32[2,4096]{1,0:T(2,128)} custom-call(bf16[32,8,128]{2,1,0:T(8,128)(2,1)S(1)} %all_to_all.16.returned_ref, s32[1,4096]{1,0:T(1,128)S(1)} %bitcast.3, s32[1,4096]{1,0:T(1,128)S(1)} %copy-done.13, bf16[256,4096]{1,0:T(8,128)(2,1)S(1)} %get-tuple-element.14.slots_ref), custom_call_target="tpu_custom_call" | custom-call | flops 4294967296 | bytes 1048576 | tf_op jit(solution)/shard_map/pallas_call | solution.py:393
Async XLA Ops:
  0.0 0.8 %copy-start = (f32[1,2,2,2048]{3,2,1,0:T(2,128)S(1)}, f32[1,2,2,2048]{3,2,1,0:T(2,128)}, u32[]{:S(2)}) copy-start(f32[1,2,2,2048]{3,2,1,0:T(2,128)} %facets_ref.1) | copy-start | bytes 98308
  1.5 15.1 %all-to-all-start = ((f32[8,64,128]{2,1,0:T(8,128)}), f32[8,64,128]{2,1,0:T(8,128)S(1)}, u32[]{:S(2)}, u32[]{:S(2)}) async-start(f32[8,64,128]{2,1,0:T(8,128)} %shard_map.118), calls=%async_computation | async-start | bytes 524288 | tf_op jit(solution)/shard_map/all_to_all | solution.py:414
  9.7 0.8 %copy-start.1 = (f32[2,4096]{1,0:T(2,128)S(1)}, f32[2,4096]{1,0:T(2,128)}, u32[]{:S(2)}) copy-start(f32[2,4096]{1,0:T(2,128)} %coords_ref.1) | copy-start | bytes 98308
  10.5 0.7 %copy-start.2 = (s32[4096,1]{0,1:T(1,128)S(1)}, s32[4096,1]{0,1:T(1,128)}, u32[]{:S(2)}) copy-start(s32[4096,1]{0,1:T(1,128)} %param.16) | copy-start | bytes 49156
  11.2 1.0 %copy-start.6 = (f32[256,2,256]{2,1,0:T(2,128)S(1)}, f32[256,2,256]{2,1,0:T(2,128)}, u32[]{:S(2)}) copy-start(f32[256,2,256]{2,1,0:T(2,128)} %constant.26.clone.inner_ref) | copy-start | bytes 1572868
  12.2 4.3 %copy-start.4 = (f32[2048]{0:T(1024)S(1)}, f32[2048]{0:T(1024)}, u32[]{:S(2)}) copy-start(f32[2048]{0:T(1024)} %param.13) | copy-start | bytes 24580
  12.2 4.3 %copy-start.5 = (f32[2,256,256]{2,1,0:T(8,128)S(1)}, f32[2,256,256]{2,1,0:T(8,128)}, u32[]{:S(2)}) copy-start(f32[2,256,256]{2,1,0:T(8,128)} %constant.29.clone.twiddle_ref) | copy-start | bytes 1572868
  12.2 4.3 %copy-start.8 = (bf16[128,512]{1,0:T(8,128)(2,1)S(1)}, bf16[128,512]{1,0:T(8,128)(2,1)}, u32[]{:S(2)}) copy-start(bf16[128,512]{1,0:T(8,128)(2,1)} %constant.28.clone.outer_l) | copy-start | bytes 393220
  12.3 4.3 %copy-start.9 = (bf16[128,512]{1,0:T(8,128)(2,1)S(1)}, bf16[128,512]{1,0:T(8,128)(2,1)}, u32[]{:S(2)}) copy-start(bf16[128,512]{1,0:T(8,128)(2,1)} %constant.27.clone.outer_h) | copy-start | bytes 393220
  15.5 0.6 %copy-start.12 = (s32[1,4096]{1,0:T(1,128)}, s32[1,4096]{1,0:T(1,128)S(1)}, u32[]{:S(2)}) copy-start(s32[1,4096]{1,0:T(1,128)S(1)} %get-tuple-element.13.position_ref) | copy-start | bytes 49156
  16.6 22.7 %copy-start.7 = (bf16[256,384]{1,0:T(8,128)(2,1)S(1)}, bf16[256,384]{1,0:T(8,128)(2,1)}, u32[]{:S(2)}) copy-start(bf16[256,384]{1,0:T(8,128)(2,1)} %constant.30.clone.cells_ref) | copy-start | bytes 589828
  16.6 22.7 %copy-start.10 = (bf16[128,128]{1,0:T(8,128)(2,1)S(1)}, bf16[128,128]{1,0:T(8,128)(2,1)}, u32[]{:S(2)}) copy-start(bf16[128,128]{1,0:T(8,128)(2,1)} %constant.32.clone.with_sin_ref) | copy-start | bytes 98308
  16.6 22.6 %copy-start.11 = (bf16[128,128]{1,0:T(8,128)(2,1)S(1)}, bf16[128,128]{1,0:T(8,128)(2,1)}, u32[]{:S(2)}) copy-start(bf16[128,128]{1,0:T(8,128)(2,1)} %constant.31.clone.with_cos_ref) | copy-start | bytes 98308
  39.3 17.7 %copy-start.3 = (s32[4096,1]{0,1:T(1,128)S(1)}, s32[4096,1]{0,1:T(1,128)}, u32[]{:S(2)}) copy-start(s32[4096,1]{0,1:T(1,128)} %param.16) | copy-start | bytes 49156
  39.3 17.7 %copy-start.13 = (s32[1,4096]{1,0:T(1,128)S(1)}, s32[1,4096]{1,0:T(1,128)}, u32[]{:S(2)}) copy-start(s32[1,4096]{1,0:T(1,128)} %copy-done.12) | copy-start | bytes 49156

commit v6 on v5

--- a/solution.py
+++ b/solution.py
@@ -112,11 +112,15 @@
     return lax.broadcasted_iota(jnp.int32, shape, axis)
 
 
+def window_start(offsets_ref, s):
+    return offsets_ref[lax.axis_index("facet") * SUBS + s]
+
+
 def pack_kernel(
-    starts_ref, coords_ref, owners_ref, inner_ref, packed_ref, position_ref, slots_ref, high_ref, low_ref, chosen
+    offsets_ref, coords_ref, owners_ref, inner_ref, packed_ref, position_ref, slots_ref, high_ref, low_ref, chosen
 ):
     for s in range(SUBS):
-        run = starts_ref[s] // 256
+        run = window_start(offsets_ref, s) // 256
         chosen[4 * s : 4 * s + 2, :] = inner_ref[run]
         chosen[4 * s + 2 : 4 * s + 4, :] = inner_ref[(run + 1) % 256]
     high_ref[...], low_ref[...] = split_in_kernel(chosen[...])
@@ -185,7 +189,7 @@
 
 
 def window_kernel(
-    starts_ref,
+    offsets_ref,
     image_ref,
     taper_ref,
     packed_ref,
@@ -218,7 +222,7 @@
     runs = split_dot((chosen_h[...], chosen_l[...]), split_in_kernel(both))
     lane = iota((2, 1024), 1) % 256
     for s in range(SUBS):
-        low = starts_ref[s] % 256
+        low = window_start(offsets_ref, s) % 256
         mine = runs[4 * s : 4 * s + 4]
         mine = jnp.where(lane >= low, mine[0:2], mine[2:4])
         real = mine[0:1, :512] - mine[1:2, 512:]
@@ -402,7 +406,6 @@
 
 
 def per_device(facets, taper_weight, offsets, point_coords, owners):
-    facet_index = lax.axis_index("facet")
     image = call(
         spread_kernel,
         jax.ShapeDtypeStruct((8, 64, 128), F32),
@@ -413,7 +416,6 @@
     )
     image = lax.all_to_all(image, "facet", split_axis=0, concat_axis=0, tiled=True)
     owner_row = owners.reshape(1, DEV_ROWS)
-    starts = lax.dynamic_slice(offsets, (facet_index * SUBS,), (SUBS,))
     inner, tables = transform_tables()
     packed, position, slots, chosen_h, chosen_l = call(
         pack_kernel,
@@ -427,7 +429,7 @@
         [smem()] + [vmem()] * 3,
         [pltpu.VMEM((128, 256), F32)],
         1 << 32,
-        starts,
+        offsets,
         point_coords,
         owner_row,
         inner,
@@ -438,7 +440,7 @@
         [smem()] + [vmem()] * 8,
         [pltpu.VMEM((2, 128, 256), F32), pltpu.VMEM((SUBS, 24, 128), F32)],
         1 << 32,
-        starts,
+        offsets,
         image,
         taper_weight.reshape(16, 128),
         packed,

time: 58.7 us -> 58.7 us (level)
    dynamic_slice x1 -> x0, local copies, waits for them, and re-layouts: 0.75 us -> none  [per_device(): starts = lax.dynamic_slice(offsets, (facet_index * SUBS,), (SUBS,))]
    unnamed x28 -> x32, local copies, waits for them, and re-layouts: 3.92 us -> 4.6 us
  transfers between devices with their start and end apart: 1 -> 1, of which waited for: 1 -> 1; matrix products, arithmetic and copies ran while one was open for 1% -> 0% of each run, Pallas kernels for 6% -> 6%
where the time goes in v6:
time: 58.7 us; the launch traced here: 58.2 us
  blocking collectives  32.8 us (56%)
  Pallas kernels  12.7 us (22%)
  starting transfers between devices  7.48 us (13%)
  local copies, waits for them, and re-layouts  4.6 us (8%)
    all_to_all x1, blocking collectives, per_device(): lax.all_to_all(payload, 'sub', split_axis=0, concat_axis=0, tiled=True)  20.9 us
    pallas_call x5, Pallas kernels, call(): pl.pallas_call(kernel, out_shape=out_shape, in_specs=in_specs, out_specs=...  12.7 us
    all_to_all x1, blocking collectives, per_device(): lax.all_to_all(values, 'sub', split_axis=0, concat_axis=0, tiled=True)  11.9 us
    all_to_all x1, starting transfers between devices, per_device(): lax.all_to_all(image, 'facet', split_axis=0, concat_axis=0, tiled=True)  7.48 us
    unnamed x32, local copies, waits for them, and re-layouts  4.6 us
  transfers between devices with their start and end apart: 1, of which 1 were waited for; matrix products, arithmetic and copies ran while one was open for 0% of the time, Pallas kernels for 6%

profile of v6, /device:TPU:1, one launch (start us, length us, event | category | flops | bytes accessed | tf_op | source)
XLA Modules:
  0.0 58.2 jit_solution(8778549486816239894)
XLA Ops:
  0.0 0.0 copy-start
  0.0 0.8 %copy-done = f32[1,2,2,2048]{3,2,1,0:T(2,128)S(1)} copy-done((f32[1,2,2,2048]{3,2,1,0:T(2,128)S(1)}, f32[1,2,2,2048]{3,2,1,0:T(2,128)}, u32[]{:S(2)}) %copy-start) | copy-done | bytes 32792
  0.8 0.7 %shard_map.118 = f32[8,64,128]{2,1,0:T(8,128)} custom-call(f32[1,2,2,2048]{3,2,1,0:T(2,128)S(1)} %copy-done), custom_call_target="tpu_custom_call" | custom-call | bytes 1048576 | tf_op jit(solution)/shard_map/pallas_call | solution.py:397
  1.5 7.5 %all-to-all-start = ((f32[8,64,128]{2,1,0:T(8,128)}), f32[8,64,128]{2,1,0:T(8,128)S(1)}, u32[]{:S(2)}, u32[]{:S(2)}) async-start(f32[8,64,128]{2,1,0:T(8,128)} %shard_map.118), calls=%async_computation | async-start | bytes 524288 | tf_op jit(solution)/shard_map/all_to_all | solution.py:417
  9.0 0.0 copy-start.1
  9.0 0.8 %copy-done.1 = f32[2,4096]{1,0:T(2,128)S(1)} copy-done((f32[2,4096]{1,0:T(2,128)S(1)}, f32[2,4096]{1,0:T(2,128)}, u32[]{:S(2)}) %copy-start.1) | copy-done | bytes 32792
  9.7 0.0 copy-start.2
  9.7 0.7 %copy-done.2 = s32[4096,1]{0,1:T(1,128)S(1)} copy-done((s32[4096,1]{0,1:T(1,128)S(1)}, s32[4096,1]{0,1:T(1,128)}, u32[]{:S(2)}) %copy-start.2) | copy-done | bytes 16408
  10.5 0.0 copy-start.5
  10.5 0.7 %copy-done.5 = s32[256]{0:T(256)S(1)} copy-done((s32[256]{0:T(256)S(1)}, s32[256]{0:T(256)}, u32[]{:S(2)}) %copy-start.5) | copy-done | bytes 1048
  11.1 0.0 copy-start.8
  11.1 1.0 %copy-done.8 = f32[256,2,256]{2,1,0:T(2,128)S(1)} copy-done((f32[256,2,256]{2,1,0:T(2,128)S(1)}, f32[256,2,256]{2,1,0:T(2,128)}, u32[]{:S(2)}) %copy-start.8) | copy-done | bytes 524312
  12.2 0.0 copy-start.4
  12.2 0.0 copy-start.6
  12.2 0.0 copy-start.7
  12.2 0.0 copy-start.10
  12.2 0.0 copy-start.11
  12.2 3.3 %shard_map.119 = (f32[32,16,128]{2,1,0:T(8,128)S(1)}, s32[1,4096]{1,0:T(1,128)S(1)}, bf16[256,4096]{1,0:T(8,128)(2,1)S(1)}, bf16[128,256]{1,0:T(8,128)(2,1)S(1)}, bf16[128,256]{1,0:T(8,128)(2,1)S(1)}) custom-call(s32[256]{0:T(256)S(1)} %copy-done.5, f32[2,4096]{1,0:T(2,128)S(1)} %copy-done.1, s32[1,4096]{1,0:T(1,128)S(1)} %bitcast.2, ...), custom_call_target="tpu_custom_call" | custom-call | flops 4294967296 | bytes 1048576 | tf_op jit(solution)/shard_map/pallas_call | solution.py:397
  15.5 0.0 copy-start.14
  15.5 0.6 %copy-done.14 = s32[1,4096]{1,0:T(1,128)} copy-done((s32[1,4096]{1,0:T(1,128)}, s32[1,4096]{1,0:T(1,128)S(1)}, u32[]{:S(2)}) %copy-start.14) | copy-done | bytes 16408
  16.1 0.5 all-to-all-done.image_ref
  16.6 0.0 copy-done.4
  16.6 0.0 copy-done.6
  16.6 0.0 copy-done.7
  16.6 0.0 copy-done.10
  16.6 0.0 copy-done.11
  16.6 0.0 copy-start.9
  16.6 0.0 copy-start.12
  16.6 0.0 copy-start.13
  16.6 1.7 %shard_map.120 = bf16[32,24,128]{2,1,0:T(8,128)(2,1)S(1)} custom-call(s32[256]{0:T(256)S(1)} %copy-done.6, f32[8,64,128]{2,1,0:T(8,128)S(1)} %all-to-all-done.image_ref, f32[16,128]{1,0:T(8,128)S(1)} %bitcast.4, f32[32,16,128]{2,1,0:T(8,128)S(1)} %get-tuple-element.10.packed_ref, bf16[128,256]{1,0:T(8,128)(2,1)S(1)} %get-tuple-element.11.chosen_h, ...), custom_call_target="tpu_custom_call" | custom-call | flops 4294967296 | bytes 1048576 | tf_op jit(solution)/shard_map/pallas_call | solution.py:397
  18.4 20.9 %all_to_all.15.arrived_ref = bf16[32,24,128]{2,1,0:T(8,128)(2,1)S(1)} all-to-all(bf16[32,24,128]{2,1,0:T(8,128)(2,1)S(1)} %shard_map.120), channel_id=1, replica_groups=mesh['facet'=8,'sub'=32] {'sub'}, dimensions={0} | all-to-all | bytes 393216 | tf_op jit(solution)/shard_map/all_to_all | solution.py:451
  39.3 0.0 copy-done.9
  39.3 0.0 copy-done.12
  39.3 0.0 copy-done.13
  39.3 0.0 copy-start.3
  39.3 0.0 copy-start.15
  39.3 5.8 %shard_map.121 = bf16[32,8,128]{2,1,0:T(8,128)(2,1)S(1)} custom-call(bf16[32,24,128]{2,1,0:T(8,128)(2,1)S(1)} %all_to_all.15.arrived_ref, bf16[256,384]{1,0:T(8,128)(2,1)S(1)} %copy-done.9, bf16[128,128]{1,0:T(8,128)(2,1)S(1)} %copy-done.13, bf16[128,128]{1,0:T(8,128)(2,1)S(1)} %copy-done.12), custom_call_target="tpu_custom_call" | custom-call | flops 4294967296 | bytes 1048576 | tf_op jit(solution)/shard_map/pallas_call | solution.py:397
  45.1 11.9 %all_to_all.16.returned_ref = bf16[32,8,128]{2,1,0:T(8,128)(2,1)S(1)} all-to-all(bf16[32,8,128]{2,1,0:T(8,128)(2,1)S(1)} %shard_map.121), channel_id=1, replica_groups=mesh['facet'=8,'sub'=32] {'sub'}, dimensions={0} | all-to-all | bytes 131072 | tf_op jit(solution)/shard_map/all_to_all | solution.py:469
  57.0 0.0 copy-done.3
  57.0 0.0 copy-done.15
  57.0 1.2 %shard_map.122 = f32[2,4096]{1,0:T(2,128)} custom-call(bf16[32,8,128]{2,1,0:T(8,128)(2,1)S(1)} %all_to_all.16.returned_ref, s32[1,4096]{1,0:T(1,128)S(1)} %bitcast.3, s32[1,4096]{1,0:T(1,128)S(1)} %copy-done.15, bf16[256,4096]{1,0:T(8,128)(2,1)S(1)} %get-tuple-element.14.slots_ref), custom_call_target="tpu_custom_call" | custom-call | flops 4294967296 | bytes 1048576 | tf_op jit(solution)/shard_map/pallas_call | solution.py:397
Async XLA Ops:
  0.0 0.8 %copy-start = (f32[1,2,2,2048]{3,2,1,0:T(2,128)S(1)}, f32[1,2,2,2048]{3,2,1,0:T(2,128)}, u32[]{:S(2)}) copy-start(f32[1,2,2,2048]{3,2,1,0:T(2,128)} %facets_ref.1) | copy-start | bytes 98308
  1.5 15.1 %all-to-all-start = ((f32[8,64,128]{2,1,0:T(8,128)}), f32[8,64,128]{2,1,0:T(8,128)S(1)}, u32[]{:S(2)}, u32[]{:S(2)}) async-start(f32[8,64,128]{2,1,0:T(8,128)} %shard_map.118), calls=%async_computation | async-start | bytes 524288 | tf_op jit(solution)/shard_map/all_to_all | solution.py:417
  9.0 0.8 %copy-start.1 = (f32[2,4096]{1,0:T(2,128)S(1)}, f32[2,4096]{1,0:T(2,128)}, u32[]{:S(2)}) copy-start(f32[2,4096]{1,0:T(2,128)} %coords_ref.1) | copy-start | bytes 98308
  9.7 0.7 %copy-start.2 = (s32[4096,1]{0,1:T(1,128)S(1)}, s32[4096,1]{0,1:T(1,128)}, u32[]{:S(2)}) copy-start(s32[4096,1]{0,1:T(1,128)} %param.16) | copy-start | bytes 49156
  10.5 0.7 %copy-start.5 = (s32[256]{0:T(256)S(1)}, s32[256]{0:T(256)}, u32[]{:S(2)}) copy-start(s32[256]{0:T(256)} %offsets_ref.3) | copy-start | bytes 3076
  11.1 1.0 %copy-start.8 = (f32[256,2,256]{2,1,0:T(2,128)S(1)}, f32[256,2,256]{2,1,0:T(2,128)}, u32[]{:S(2)}) copy-start(f32[256,2,256]{2,1,0:T(2,128)} %constant.14.clone.inner_ref) | copy-start | bytes 1572868
  12.2 4.4 %copy-start.4 = (f32[2048]{0:T(1024)S(1)}, f32[2048]{0:T(1024)}, u32[]{:S(2)}) copy-start(f32[2048]{0:T(1024)} %param.13) | copy-start | bytes 24580
  12.2 4.4 %copy-start.6 = (s32[256]{0:T(256)S(1)}, s32[256]{0:T(256)}, u32[]{:S(2)}) copy-start(s32[256]{0:T(256)} %offsets_ref.3) | copy-start | bytes 3076
  12.2 4.4 %copy-start.7 = (f32[2,256,256]{2,1,0:T(8,128)S(1)}, f32[2,256,256]{2,1,0:T(8,128)}, u32[]{:S(2)}) copy-start(f32[2,256,256]{2,1,0:T(8,128)} %constant.17.clone.twiddle_ref) | copy-start | bytes 1572868
  12.2 4.4 %copy-start.10 = (bf16[128,512]{1,0:T(8,128)(2,1)S(1)}, bf16[128,512]{1,0:T(8,128)(2,1)}, u32[]{:S(2)}) copy-start(bf16[128,512]{1,0:T(8,128)(2,1)} %constant.16.clone.outer_l) | copy-start | bytes 393220
  12.2 4.4 %copy-start.11 = (bf16[128,512]{1,0:T(8,128)(2,1)S(1)}, bf16[128,512]{1,0:T(8,128)(2,1)}, u32[]{:S(2)}) copy-start(bf16[128,512]{1,0:T(8,128)(2,1)} %constant.15.clone.outer_h) | copy-start | bytes 393220
  15.5 0.6 %copy-start.14 = (s32[1,4096]{1,0:T(1,128)}, s32[1,4096]{1,0:T(1,128)S(1)}, u32[]{:S(2)}) copy-start(s32[1,4096]{1,0:T(1,128)S(1)} %get-tuple-element.13.position_ref) | copy-start | bytes 49156
  16.6 22.7 %copy-start.9 = (bf16[256,384]{1,0:T(8,128)(2,1)S(1)}, bf16[256,384]{1,0:T(8,128)(2,1)}, u32[]{:S(2)}) copy-start(bf16[256,384]{1,0:T(8,128)(2,1)} %constant.18.clone.cells_ref) | copy-start | bytes 589828
  16.6 22.7 %copy-start.12 = (bf16[128,128]{1,0:T(8,128)(2,1)S(1)}, bf16[128,128]{1,0:T(8,128)(2,1)}, u32[]{:S(2)}) copy-start(bf16[128,128]{1,0:T(8,128)(2,1)} %constant.20.clone.with_sin_ref) | copy-start | bytes 98308
  16.6 22.7 %copy-start.13 = (bf16[128,128]{1,0:T(8,128)(2,1)S(1)}, bf16[128,128]{1,0:T(8,128)(2,1)}, u32[]{:S(2)}) copy-start(bf16[128,128]{1,0:T(8,128)(2,1)} %constant.19.clone.with_cos_ref) | copy-start | bytes 98308
  39.3 17.7 %copy-start.3 = (s32[4096,1]{0,1:T(1,128)S(1)}, s32[4096,1]{0,1:T(1,128)}, u32[]{:S(2)}) copy-start(s32[4096,1]{0,1:T(1,128)} %param.16) | copy-start | bytes 49156
  39.3 17.7 %copy-start.15 = (s32[1,4096]{1,0:T(1,128)S(1)}, s32[1,4096]{1,0:T(1,128)}, u32[]{:S(2)}) copy-start(s32[1,4096]{1,0:T(1,128)} %copy-done.14) | copy-start | bytes 49156

commit v7 on v6

--- a/solution.py
+++ b/solution.py
@@ -213,9 +213,11 @@
                     columns[r, at : at + 8, 128 * side : 128 * side + 128] = (
                         line * taper_ref[pl.ds(side, 8, stride=2), :]
                     )
-        mixed = split_dot(split_in_kernel(columns[r].T), (outer_h[...], outer_l[...]))
-        real, imag = mixed[:, :256], mixed[:, 256:]
-        turn_real, turn_imag = twiddle_ref[0], twiddle_ref[1]
+    by_column = jnp.concatenate([columns[0].T, columns[1].T], axis=0)
+    mixed = split_dot(split_in_kernel(by_column), (outer_h[...], outer_l[...]))
+    turn_real, turn_imag = twiddle_ref[0], twiddle_ref[1]
+    for r in range(2):
+        real, imag = mixed[256 * r : 256 * r + 256, :256], mixed[256 * r : 256 * r + 256, 256:]
         reals.append(real * turn_real - imag * turn_imag)
         imags.append(real * turn_imag + imag * turn_real)
     both = jnp.concatenate(reals + imags, axis=1)

time: 58.7 us -> 58.8 us (level)
  no operation moved by 1% of the time
where the time goes in v7:
time: 58.8 us; the launch traced here: 58.3 us
  blocking collectives  32.8 us (56%)
  Pallas kernels  12.8 us (22%)
  starting transfers between devices  7.48 us (13%)
  local copies, waits for them, and re-layouts  4.6 us (8%)
    all_to_all x1, blocking collectives, per_device(): lax.all_to_all(payload, 'sub', split_axis=0, concat_axis=0, tiled=True)  20.9 us
    pallas_call x5, Pallas kernels, call(): pl.pallas_call(kernel, out_shape=out_shape, in_specs=in_specs, out_specs=...  12.8 us
    all_to_all x1, blocking collectives, per_device(): lax.all_to_all(values, 'sub', split_axis=0, concat_axis=0, tiled=True)  11.9 us
    all_to_all x1, starting transfers between devices, per_device(): lax.all_to_all(image, 'facet', split_axis=0, concat_axis=0, tiled=True)  7.48 us
    unnamed x32, local copies, waits for them, and re-layouts  4.6 us
  transfers between devices with their start and end apart: 1, of which 1 were waited for; matrix products, arithmetic and copies ran while one was open for 0% of the time, Pallas kernels for 6%

profile of v7, /device:TPU:1, one launch (start us, length us, event | category | flops | bytes accessed | tf_op | source)
XLA Modules:
  0.0 58.3 jit_solution(16757304741944146590)
XLA Ops:
  0.0 0.0 copy-start
  0.0 0.8 %copy-done = f32[1,2,2,2048]{3,2,1,0:T(2,128)S(1)} copy-done((f32[1,2,2,2048]{3,2,1,0:T(2,128)S(1)}, f32[1,2,2,2048]{3,2,1,0:T(2,128)}, u32[]{:S(2)}) %copy-start) | copy-done | bytes 32792
  0.8 0.7 %shard_map.118 = f32[8,64,128]{2,1,0:T(8,128)} custom-call(f32[1,2,2,2048]{3,2,1,0:T(2,128)S(1)} %copy-done), custom_call_target="tpu_custom_call" | custom-call | bytes 1048576 | tf_op jit(solution)/shard_map/pallas_call | solution.py:399
  1.5 7.5 %all-to-all-start = ((f32[8,64,128]{2,1,0:T(8,128)}), f32[8,64,128]{2,1,0:T(8,128)S(1)}, u32[]{:S(2)}, u32[]{:S(2)}) async-start(f32[8,64,128]{2,1,0:T(8,128)} %shard_map.118), calls=%async_computation | async-start | bytes 524288 | tf_op jit(solution)/shard_map/all_to_all | solution.py:419
  9.0 0.0 copy-start.1
  9.0 0.8 %copy-done.1 = f32[2,4096]{1,0:T(2,128)S(1)} copy-done((f32[2,4096]{1,0:T(2,128)S(1)}, f32[2,4096]{1,0:T(2,128)}, u32[]{:S(2)}) %copy-start.1) | copy-done | bytes 32792
  9.7 0.0 copy-start.2
  9.7 0.7 %copy-done.2 = s32[4096,1]{0,1:T(1,128)S(1)} copy-done((s32[4096,1]{0,1:T(1,128)S(1)}, s32[4096,1]{0,1:T(1,128)}, u32[]{:S(2)}) %copy-start.2) | copy-done | bytes 16408
  10.5 0.0 copy-start.5
  10.5 0.7 %copy-done.5 = s32[256]{0:T(256)S(1)} copy-done((s32[256]{0:T(256)S(1)}, s32[256]{0:T(256)}, u32[]{:S(2)}) %copy-start.5) | copy-done | bytes 1048
  11.1 0.0 copy-start.8
  11.1 1.0 %copy-done.8 = f32[256,2,256]{2,1,0:T(2,128)S(1)} copy-done((f32[256,2,256]{2,1,0:T(2,128)S(1)}, f32[256,2,256]{2,1,0:T(2,128)}, u32[]{:S(2)}) %copy-start.8) | copy-done | bytes 524312
  12.2 0.0 copy-start.4
  12.2 0.0 copy-start.6
  12.2 0.0 copy-start.7
  12.2 0.0 copy-start.10
  12.2 0.0 copy-start.11
  12.2 3.3 %shard_map.119 = (f32[32,16,128]{2,1,0:T(8,128)S(1)}, s32[1,4096]{1,0:T(1,128)S(1)}, bf16[256,4096]{1,0:T(8,128)(2,1)S(1)}, bf16[128,256]{1,0:T(8,128)(2,1)S(1)}, bf16[128,256]{1,0:T(8,128)(2,1)S(1)}) custom-call(s32[256]{0:T(256)S(1)} %copy-done.5, f32[2,4096]{1,0:T(2,128)S(1)} %copy-done.1, s32[1,4096]{1,0:T(1,128)S(1)} %bitcast.2, ...), custom_call_target="tpu_custom_call" | custom-call | flops 4294967296 | bytes 1048576 | tf_op jit(solution)/shard_map/pallas_call | solution.py:399
  15.5 0.0 copy-start.14
  15.5 0.6 %copy-done.14 = s32[1,4096]{1,0:T(1,128)} copy-done((s32[1,4096]{1,0:T(1,128)}, s32[1,4096]{1,0:T(1,128)S(1)}, u32[]{:S(2)}) %copy-start.14) | copy-done | bytes 16408
  16.1 0.5 all-to-all-done.image_ref
  16.6 0.0 copy-done.4
  16.6 0.0 copy-done.6
  16.6 0.0 copy-done.7
  16.6 0.0 copy-done.10
  16.6 0.0 copy-done.11
  16.6 0.0 copy-start.9
  16.6 0.0 copy-start.12
  16.6 0.0 copy-start.13
  16.6 1.8 %shard_map.120 = bf16[32,24,128]{2,1,0:T(8,128)(2,1)S(1)} custom-call(s32[256]{0:T(256)S(1)} %copy-done.6, f32[8,64,128]{2,1,0:T(8,128)S(1)} %all-to-all-done.image_ref, f32[16,128]{1,0:T(8,128)S(1)} %bitcast.4, f32[32,16,128]{2,1,0:T(8,128)S(1)} %get-tuple-element.10.packed_ref, bf16[128,256]{1,0:T(8,128)(2,1)S(1)} %get-tuple-element.11.chosen_h, ...), custom_call_target="tpu_custom_call" | custom-call | flops 4294967296 | bytes 1048576 | tf_op jit(solution)/shard_map/pallas_call | solution.py:399
  18.4 20.9 %all_to_all.15.arrived_ref = bf16[32,24,128]{2,1,0:T(8,128)(2,1)S(1)} all-to-all(bf16[32,24,128]{2,1,0:T(8,128)(2,1)S(1)} %shard_map.120), channel_id=1, replica_groups=mesh['facet'=8,'sub'=32] {'sub'}, dimensions={0} | all-to-all | bytes 393216 | tf_op jit(solution)/shard_map/all_to_all | solution.py:453
  39.3 0.0 copy-done.9
  39.3 0.0 copy-done.12
  39.3 0.0 copy-done.13
  39.3 0.0 copy-start.3
  39.3 0.0 copy-start.15
  39.3 5.8 %shard_map.121 = bf16[32,8,128]{2,1,0:T(8,128)(2,1)S(1)} custom-call(bf16[32,24,128]{2,1,0:T(8,128)(2,1)S(1)} %all_to_all.15.arrived_ref, bf16[256,384]{1,0:T(8,128)(2,1)S(1)} %copy-done.9, bf16[128,128]{1,0:T(8,128)(2,1)S(1)} %copy-done.13, bf16[128,128]{1,0:T(8,128)(2,1)S(1)} %copy-done.12), custom_call_target="tpu_custom_call" | custom-call | flops 4294967296 | bytes 1048576 | tf_op jit(solution)/shard_map/pallas_call | solution.py:399
  45.1 11.9 %all_to_all.16.returned_ref = bf16[32,8,128]{2,1,0:T(8,128)(2,1)S(1)} all-to-all(bf16[32,8,128]{2,1,0:T(8,128)(2,1)S(1)} %shard_map.121), channel_id=1, replica_groups=mesh['facet'=8,'sub'=32] {'sub'}, dimensions={0} | all-to-all | bytes 131072 | tf_op jit(solution)/shard_map/all_to_all | solution.py:471
  57.0 0.0 copy-done.3
  57.0 0.0 copy-done.15
  57.0 1.2 %shard_map.122 = f32[2,4096]{1,0:T(2,128)} custom-call(bf16[32,8,128]{2,1,0:T(8,128)(2,1)S(1)} %all_to_all.16.returned_ref, s32[1,4096]{1,0:T(1,128)S(1)} %bitcast.3, s32[1,4096]{1,0:T(1,128)S(1)} %copy-done.15, bf16[256,4096]{1,0:T(8,128)(2,1)S(1)} %get-tuple-element.14.slots_ref), custom_call_target="tpu_custom_call" | custom-call | flops 4294967296 | bytes 1048576 | tf_op jit(solution)/shard_map/pallas_call | solution.py:399
Async XLA Ops:
  0.0 0.8 %copy-start = (f32[1,2,2,2048]{3,2,1,0:T(2,128)S(1)}, f32[1,2,2,2048]{3,2,1,0:T(2,128)}, u32[]{:S(2)}) copy-start(f32[1,2,2,2048]{3,2,1,0:T(2,128)} %facets_ref.1) | copy-start | bytes 98308
  1.5 15.1 %all-to-all-start = ((f32[8,64,128]{2,1,0:T(8,128)}), f32[8,64,128]{2,1,0:T(8,128)S(1)}, u32[]{:S(2)}, u32[]{:S(2)}) async-start(f32[8,64,128]{2,1,0:T(8,128)} %shard_map.118), calls=%async_computation | async-start | bytes 524288 | tf_op jit(solution)/shard_map/all_to_all | solution.py:419
  9.0 0.8 %copy-start.1 = (f32[2,4096]{1,0:T(2,128)S(1)}, f32[2,4096]{1,0:T(2,128)}, u32[]{:S(2)}) copy-start(f32[2,4096]{1,0:T(2,128)} %coords_ref.1) | copy-start | bytes 98308
  9.7 0.7 %copy-start.2 = (s32[4096,1]{0,1:T(1,128)S(1)}, s32[4096,1]{0,1:T(1,128)}, u32[]{:S(2)}) copy-start(s32[4096,1]{0,1:T(1,128)} %param.16) | copy-start | bytes 49156
  10.5 0.7 %copy-start.5 = (s32[256]{0:T(256)S(1)}, s32[256]{0:T(256)}, u32[]{:S(2)}) copy-start(s32[256]{0:T(256)} %offsets_ref.3) | copy-start | bytes 3076
  11.1 1.0 %copy-start.8 = (f32[256,2,256]{2,1,0:T(2,128)S(1)}, f32[256,2,256]{2,1,0:T(2,128)}, u32[]{:S(2)}) copy-start(f32[256,2,256]{2,1,0:T(2,128)} %constant.14.clone.inner_ref) | copy-start | bytes 1572868
  12.2 4.4 %copy-start.4 = (f32[2048]{0:T(1024)S(1)}, f32[2048]{0:T(1024)}, u32[]{:S(2)}) copy-start(f32[2048]{0:T(1024)} %param.13) | copy-start | bytes 24580
  12.2 4.4 %copy-start.6 = (s32[256]{0:T(256)S(1)}, s32[256]{0:T(256)}, u32[]{:S(2)}) copy-start(s32[256]{0:T(256)} %offsets_ref.3) | copy-start | bytes 3076
  12.2 4.4 %copy-start.7 = (f32[2,256,256]{2,1,0:T(8,128)S(1)}, f32[2,256,256]{2,1,0:T(8,128)}, u32[]{:S(2)}) copy-start(f32[2,256,256]{2,1,0:T(8,128)} %constant.17.clone.twiddle_ref) | copy-start | bytes 1572868
  12.2 4.4 %copy-start.10 = (bf16[128,512]{1,0:T(8,128)(2,1)S(1)}, bf16[128,512]{1,0:T(8,128)(2,1)}, u32[]{:S(2)}) copy-start(bf16[128,512]{1,0:T(8,128)(2,1)} %constant.16.clone.outer_l) | copy-start | bytes 393220
  12.2 4.4 %copy-start.11 = (bf16[128,512]{1,0:T(8,128)(2,1)S(1)}, bf16[128,512]{1,0:T(8,128)(2,1)}, u32[]{:S(2)}) copy-start(bf16[128,512]{1,0:T(8,128)(2,1)} %constant.15.clone.outer_h) | copy-start | bytes 393220
  15.5 0.6 %copy-start.14 = (s32[1,4096]{1,0:T(1,128)}, s32[1,4096]{1,0:T(1,128)S(1)}, u32[]{:S(2)}) copy-start(s32[1,4096]{1,0:T(1,128)S(1)} %get-tuple-element.13.position_ref) | copy-start | bytes 49156
  16.6 22.7 %copy-start.9 = (bf16[256,384]{1,0:T(8,128)(2,1)S(1)}, bf16[256,384]{1,0:T(8,128)(2,1)}, u32[]{:S(2)}) copy-start(bf16[256,384]{1,0:T(8,128)(2,1)} %constant.18.clone.cells_ref) | copy-start | bytes 589828
  16.6 22.7 %copy-start.12 = (bf16[128,128]{1,0:T(8,128)(2,1)S(1)}, bf16[128,128]{1,0:T(8,128)(2,1)}, u32[]{:S(2)}) copy-start(bf16[128,128]{1,0:T(8,128)(2,1)} %constant.20.clone.with_sin_ref) | copy-start | bytes 98308
  16.6 22.7 %copy-start.13 = (bf16[128,128]{1,0:T(8,128)(2,1)S(1)}, bf16[128,128]{1,0:T(8,128)(2,1)}, u32[]{:S(2)}) copy-start(bf16[128,128]{1,0:T(8,128)(2,1)} %constant.19.clone.with_cos_ref) | copy-start | bytes 98308
  39.3 17.7 %copy-start.3 = (s32[4096,1]{0,1:T(1,128)S(1)}, s32[4096,1]{0,1:T(1,128)}, u32[]{:S(2)}) copy-start(s32[4096,1]{0,1:T(1,128)} %param.16) | copy-start | bytes 49156
  39.3 17.7 %copy-start.15 = (s32[1,4096]{1,0:T(1,128)S(1)}, s32[1,4096]{1,0:T(1,128)}, u32[]{:S(2)}) copy-start(s32[1,4096]{1,0:T(1,128)} %copy-done.14) | copy-start | bytes 49156
